TPU v7x, 768 devices: a whole 4x8x12 slice. The times are simulated.
768 devices in a mesh: dp: 2 (over core), seq: 4 (over x), tensor: 96 (over y, z).
Axes of the slice: x: 4, y: 8, z: 12, core: 2. Of those that a mesh axis runs over, the one named last changes fastest.
Arguments:
- inputs: bfloat16 [1024, 12288], P(('dp', 'seq')), may hold values from -6 to 6
- out_grad: bfloat16 [1024, 12288], P(('dp', 'seq')), may hold values from -6 to 6
- up_blocks: bfloat16 [192, 24, 128, 128], P('tensor'), may hold values from -0.109375 to 0.109375
- down_blocks: bfloat16 [192, 24, 128, 128], P('tensor'), may hold values from -0.09375 to 0.09375
- up_rows: int32 [192, 24], P('tensor'), may hold values from 0 to 95, as said below
- down_cols: int32 [192, 24], P('tensor'), may hold values from 0 to 95, as said below
- slot_count: int32 [96], P('tensor'), may hold values from 1 to 2, as said below
Outputs:
- input_grad: bfloat16 [1024, 12288], P(('dp', 'seq'), 'tensor')
- up_grad: bfloat16 [192, 24, 128, 128], P('tensor', ('dp', 'seq'))
- down_grad: bfloat16 [192, 24, 128, 128], P('tensor', ('dp', 'seq'))
Inputs may be any that keep to these rules, and one draw needn't show every extreme that they name: `up_rows`: each row names 24 different block numbers. `down_cols`: each row names 24 different block numbers. `slot_count`: half of the owners hold 1 and half hold 2; the counts sum to 144. Slots at or beyond an owner's count hold no hidden block.
All inputs are finite; a program needn't handle non-finite values.
Results may differ from a plain program's by a relative error of at most 0.017.
Values may be sent and summed in bfloat16 or wider, within the bound.
No kernel may reach another device: no remote copies, remote signals or barrier semaphores. Data moves between devices by JAX's collectives and lax.ppermute only.
A program may use at most 64 MiB of HBM per device.

v0:
```python
import jax
import jax.numpy as jnp
from jax import lax
from jax.sharding import PartitionSpec as P


def gelu_value(pre_act):
    argument = 0.7978845608 * (pre_act + 0.044715 * pre_act * pre_act * pre_act)
    return 0.5 * pre_act * (1.0 + jnp.tanh(argument))


def gelu_slope(pre_act):
    argument = 0.7978845608 * (pre_act + 0.044715 * pre_act * pre_act * pre_act)
    tangent = jnp.tanh(argument)
    return 0.5 * (1.0 + tangent) + 0.5 * pre_act * (1.0 - tangent * tangent) * 0.7978845608 * (
        1.0 + 3.0 * 0.044715 * pre_act * pre_act
    )


def input_gradient(pre_grad, up_blocks, up_rows, tok_rows, block_count, block_edge):
    slot_cap, fan_count = up_rows.shape
    flat_rows = up_rows.reshape(slot_cap * fan_count)
    products = jnp.einsum("stb,skcb->tskc", pre_grad, up_blocks, preferred_element_type=jnp.float32)
    products = products.reshape(tok_rows, slot_cap * fan_count, block_edge)
    one_hot = (flat_rows[:, None] == jnp.arange(block_count, dtype=jnp.int32)[None, :]).astype(
        jnp.float32
    )
    placed = jnp.einsum("tjc,jr->trc", products, one_hot, precision=lax.Precision.HIGHEST)
    partial_value = placed.reshape(tok_rows, block_count * block_edge)
    return lax.psum_scatter(partial_value, "tensor", scatter_dimension=1, tiled=True).astype(
        jnp.bfloat16
    )


def weight_gradients(input_taken, grad_taken, hidden, pre_grad):
    down_part = jnp.einsum("stb,tskj->skbj", hidden, grad_taken, preferred_element_type=jnp.float32)
    up_part = jnp.einsum(
        "tskc,stb->skcb", input_taken, pre_grad, preferred_element_type=jnp.float32
    )
    up_part = up_part.astype(jnp.bfloat16)
    down_part = down_part.astype(jnp.bfloat16)
    up_sum, down_sum = (
        lax.psum_scatter(up_part, ("dp", "seq"), scatter_dimension=1, tiled=True).astype(
            jnp.float32
        ),
        lax.psum_scatter(down_part, ("dp", "seq"), scatter_dimension=1, tiled=True).astype(
            jnp.float32
        ),
    )
    return (up_sum.astype(jnp.bfloat16), down_sum.astype(jnp.bfloat16))


def local(inputs, out_grad, up_blocks, down_blocks, up_rows, down_cols, slot_count):
    tok_rows, features = inputs.shape
    slot_cap = up_blocks.shape[0]
    block_edge = up_blocks.shape[2]
    block_count = features // block_edge
    live_mask = (jnp.arange(slot_cap, dtype=jnp.int32) < slot_count[0]).astype(jnp.float32)[
        :, None, None
    ]
    input_blocks = inputs.reshape(tok_rows, block_count, block_edge)
    grad_blocks = out_grad.reshape(tok_rows, block_count, block_edge)
    input_taken = input_blocks[:, up_rows, :]
    grad_taken = grad_blocks[:, down_cols, :]
    pre_act = jnp.einsum(
        "tskc,skcb->stb", input_taken, up_blocks, preferred_element_type=jnp.float32
    )
    hidden = (gelu_value(pre_act) * live_mask).astype(jnp.bfloat16)
    hid_grad = jnp.einsum(
        "tskj,skbj->stb", grad_taken, down_blocks, preferred_element_type=jnp.float32
    )
    pre_grad = (hid_grad * gelu_slope(pre_act) * live_mask).astype(jnp.bfloat16)
    input_grad = input_gradient(pre_grad, up_blocks, up_rows, tok_rows, block_count, block_edge)
    up_grad, down_grad = weight_gradients(input_taken, grad_taken, hidden, pre_grad)
    return (input_grad, up_grad, down_grad)


def solution(mesh):
    in_specs = (
        P(("dp", "seq"), None),
        P(("dp", "seq"), None),
        P("tensor", None, None, None),
        P("tensor", None, None, None),
        P("tensor", None),
        P("tensor", None),
        P("tensor"),
    )
    out_specs = (
        P(("dp", "seq"), "tensor"),
        P("tensor", ("dp", "seq"), None, None),
        P("tensor", ("dp", "seq"), None, None),
    )
    return jax.shard_map(local, mesh=mesh, in_specs=in_specs, out_specs=out_specs, check_vma=False)
```

profile of v0, /device:TPU:2, one launch (start us, length us, event | category | flops | bytes accessed | tf_op | source)
XLA Modules:
  0.0 761.4 jit_solution(4670299955045360024)
XLA Ops:
  8.8 0.7 compare_select_fusion.1
  9.5 0.1 reshape.30
  9.6 0.7 compare_select_fusion
  10.3 0.1 reshape.38
  10.4 4.6 copy.36
  15.0 4.7 copy.37
  19.7 2.7 gather_fusion.1
  22.4 1.6 copy.38
  24.0 4.7 copy.32
  28.6 4.6 copy.33
  33.3 3.9 gather_fusion
  37.1 2.6 copy.34
  39.7 0.6 convolution_bitcast_fusion
  40.3 0.8 copy-done.3
  41.1 1.9 fusion.4
  43.0 0.6 copy-done.4
  43.6 0.6 fusion.10
  44.1 0.8 copy-done.2
  45.0 1.7 convolution_convert_fusion.1
  46.7 0.2 reduce-scatter.8.cloned.1.call-start
  47.0 0.4 copy-done.5
  47.4 0.1 eq.15
  47.5 0.6 fusion.28
  48.0 4.7 fusion
  52.8 7.5 copy.60
  60.3 1.3 dynamic-slice
  62.2 74.8 %all-reduce.5.cloned.1.call-done = (bf16[2,24,128,128]{3,2,1,0:T(8,128)(2,1)}, bf16[2,24,128,128]{2,3,1,0:T(8,128)(2,1)}) async-done(((bf16[2,24,128,128]{3,2,1,0:T(8,128)(2,1)}, bf16[2,24,128,128]{2,3,1,0:T(8,128)(2,1)}), (bf16[2,24,128,128]{3,2,1,0:T(8,128)(2,1)}, bf16[2,24,128,128]{2,3,1,0:T(8,128)(2,1)})) %all-reduce.5.cloned.1.call-update) | async-done | bytes 3145744
  137.0 0.9 constant_dynamic-slice_fusion
  138.0 0.8 copy.41
  138.8 1.6 constant_dynamic-slice_fusion.1
  140.4 612.1 %reduce-scatter.8.cloned.1.call-done = f32[128,128]{1,0:T(8,128)} async-done(((f32[128,12288]{1,0:T(8,128)}), f32[128,128]{1,0:T(8,128)}) %reduce-scatter.8.cloned.1.call-update) | async-done | bytes 65552 | tf_op jit(solution)/shard_map/reduce_scatter | solution.py:30
  752.5 1.5 convert_element_type.32
  (14 shorter events, 0.1 us)
Async XLA Ops:
  8.0 31.7 %copy-start = (bf16[2,24,128,128]{3,2,1,0:T(8,128)(2,1)S(1)}, bf16[2,24,128,128]{3,2,1,0:T(8,128)(2,1)}, u32[]{:S(2)}) copy-start(bf16[2,24,128,128]{3,2,1,0:T(8,128)(2,1)} %param.9) | copy-start | bytes 4718596
  8.0 129.0 %all-reduce.5.cloned.1.call-start = ((), (), s32[]{:S(2)}) async-start(), calls=%async_computation.2 | async-start | bytes 6291456
  39.7 1.4 copy-start.3
  41.1 1.9 copy-start.1
  41.1 2.4 copy-start.4
  43.6 1.4 copy-start.2
  46.7 0.7 copy-start.5
  46.7 705.8 %reduce-scatter.8.cloned.1.call-start = ((), (), s32[]{:S(2)}) async-start(), calls=%async_computation.1 | async-start | bytes 6356992 | tf_op jit(solution)/shard_map/reduce_scatter | solution.py:30
Sparse Core Ops, SparseCore 0:
  46.8 90.1 all-reduce.4
Sparse Core Ops, SparseCore 1:
  60.4 692.0 reduce-scatter.7
where the time goes:
time: 762 us; the launch traced here: 761 us
  waiting for transfers between devices  687 us (90%)
  local copies, waits for them, and re-layouts  44.5 us (6%)
  between operations  17 us (2%)
  matrix products  9.98 us (1%)
    reduce_scatter x1, waiting for transfers between devices, input_gradient(): lax.psum_scatter(partial_value, 'tensor', scatter_dimension=1, tiled=True)  612 us
    unnamed x3, waiting for transfers between devices  74.8 us
    unnamed x19, local copies, waits for them, and re-layouts  24.2 us
  transfers between devices with their start and end apart: 2, of which 2 were waited for; matrix products, arithmetic and copies ran while one was open for 2% of the time, Pallas kernels for 0%

commit v1 on v0

v1 whole, which is shorter than its diff:
```python
import jax
import jax.numpy as jnp
from jax import lax
from jax.experimental import pallas as pl
from jax.experimental.pallas import tpu as pltpu
from jax.sharding import Mesh
from jax.sharding import PartitionSpec as P

BLK = 128
N_DP, N_SEQ, N_Y, N_Z = 2, 4, 8, 12
TOKENS_AX = ("dp", "seq")
OWNER_AX = ("ya", "yb", "yc", "za", "zb", "zc")
VMEM_LIMIT = 48 * 1024 * 1024


def gelu_pair(pre_act):
    squared = pre_act * pre_act
    tangent = jnp.tanh(0.7978845608 * (pre_act + 0.044715 * squared * pre_act))
    value = 0.5 * pre_act * (1.0 + tangent)
    slope = 0.5 * (1.0 + tangent) + 0.5 * pre_act * (1.0 - tangent * tangent) * 0.7978845608 * (
        1.0 + 3.0 * 0.044715 * squared
    )
    return value, slope


def two_blocks(ref, first, second):
    return jnp.concatenate(
        [
            ref[:, pl.ds(pl.multiple_of(first * BLK, BLK), BLK)],
            ref[:, pl.ds(pl.multiple_of(second * BLK, BLK), BLK)],
        ],
        axis=1,
    )


def dot_nn(left, right):
    return lax.dot_general(left, right, (((1,), (0,)), ((), ())), preferred_element_type=jnp.float32)


def dot_nt(left, right):
    return lax.dot_general(left, right, (((1,), (1,)), ((), ())), preferred_element_type=jnp.float32)


def place_of(r, core):
    y, z = r // N_Z, r % N_Z
    near = ((y % 2) ^ core) * 2 + ((z % 2) ^ core)
    mid = (((y // 2) % 2) ^ core) * 2 + (((z // 2) % 2) ^ core)
    return (near * 4 + mid) * 6 + (y // 4) * 3 + z // 4


def layer_kernel(core, rows, cols, count, inputs, out_grad, ups, downs, placed, parts):
    slots, fan = rows.shape
    tok = inputs.shape[0]
    each = parts.shape[3]
    placed[...] = jnp.zeros_like(placed)
    for s in range(slots):
        live = (s < count[0]).astype(jnp.float32)
        pre_act = jnp.zeros((tok, BLK), jnp.float32)
        hid_grad = jnp.zeros((tok, BLK), jnp.float32)
        for k in range(0, fan, 2):
            pre_act += dot_nn(two_blocks(inputs, rows[s, k], rows[s, k + 1]), ups[s, k * BLK : (k + 2) * BLK, :])
            hid_grad += dot_nt(
                two_blocks(out_grad, cols[s, k], cols[s, k + 1]),
                jnp.concatenate([downs[s, k * BLK : (k + 1) * BLK, :], downs[s, (k + 1) * BLK : (k + 2) * BLK, :]], axis=1),
            )
        value, slope = gelu_pair(pre_act)
        pre_grad = hid_grad * slope * live
        hidden_t = jnp.transpose(value * live).astype(jnp.bfloat16)
        pre_grad_t = jnp.transpose(pre_grad).astype(jnp.bfloat16)
        pre_grad = pre_grad.astype(jnp.bfloat16)
        for k in range(0, fan, 2):
            both = dot_nt(pre_grad, ups[s, k * BLK : (k + 2) * BLK, :])
            for i in range(2):
                at = place_of(rows[s, k + i], core[0])
                product = both[:, i * BLK : (i + 1) * BLK]
                if s > 0:
                    product += placed[at].astype(jnp.float32)
                placed[at] = product.astype(jnp.bfloat16)
        for k in range(0, fan, 2):
            up = dot_nn(pre_grad_t, two_blocks(inputs, rows[s, k], rows[s, k + 1]))
            down = dot_nn(hidden_t, two_blocks(out_grad, cols[s, k], cols[s, k + 1]))
            for i in range(2):
                piece = slice(i * BLK, (i + 1) * BLK)
                parts[(k + i) // each, 0, s, (k + i) % each] = up[:, piece].astype(jnp.bfloat16)
                parts[(k + i) // each, 1, s, (k + i) % each] = down[:, piece].astype(jnp.bfloat16)


def owner_groups(step_y, count_y, step_z, count_z):
    groups = []
    for core in range(N_DP):
        for seq in range(N_SEQ):
            for y in range(N_Y):
                for z in range(N_Z):
                    if (y // step_y) % count_y or (z // step_z) % count_z:
                        continue
                    groups.append(
                        [
                            ((core * N_SEQ + seq) * N_Y + (y + (i + core) * step_y) % N_Y) * N_Z
                            + (z + (j + core) * step_z) % N_Z
                            for i in range(count_y)
                            for j in range(count_z)
                        ]
                    )
    return groups


def sum_first(terms):
    total = terms[0].astype(jnp.float32)
    for i in range(1, terms.shape[0]):
        total += terms[i].astype(jnp.float32)
    return total.astype(jnp.bfloat16)


def local(inputs, out_grad, up_blocks, down_blocks, up_rows, down_cols, slot_count):
    tok, features = inputs.shape
    slots, fan = up_rows.shape
    groups = N_DP * N_SEQ
    each = fan // groups
    smem = pl.BlockSpec(memory_space=pltpu.SMEM)
    vmem = pl.BlockSpec(memory_space=pltpu.VMEM)
    core = lax.axis_index("dp").astype(jnp.int32).reshape(1)
    placed, parts = pl.pallas_call(
        layer_kernel,
        out_shape=(
            jax.ShapeDtypeStruct((N_Y * N_Z, tok, BLK), jnp.bfloat16),
            jax.ShapeDtypeStruct((groups, 2, slots, each, BLK, BLK), jnp.bfloat16),
        ),
        in_specs=[smem] * 4 + [vmem] * 4,
        out_specs=(vmem,) * 2,
        compiler_params=pltpu.CompilerParams(vmem_limit_bytes=VMEM_LIMIT),
    )(
        core,
        up_rows,
        down_cols,
        slot_count,
        inputs,
        out_grad,
        up_blocks.reshape(slots, fan * BLK, BLK),
        down_blocks.reshape(slots, fan * BLK, BLK),
    )
    summed = lax.psum_scatter(parts, TOKENS_AX, scatter_dimension=0)
    up_grad = jnp.swapaxes(summed[0], 2, 3)
    down_grad = summed[1]

    everyone = TOKENS_AX + OWNER_AX
    near = lax.all_to_all(
        placed.reshape(4, 24, tok, BLK), everyone, 0, 0, axis_index_groups=owner_groups(1, 2, 1, 2)
    )
    near = sum_first(near)
    mid = lax.all_to_all(near.reshape(4, 6, tok, BLK), everyone, 0, 0, axis_index_groups=owner_groups(2, 2, 2, 2))
    mid = sum_first(mid)
    far = lax.all_to_all(mid, ("ya", "za"), 0, 0)
    input_grad = sum_first(far)
    return input_grad, up_grad, down_grad


def solution(mesh):
    split = Mesh(mesh.devices.reshape(N_DP, N_SEQ, 2, 2, 2, 3, 2, 2), TOKENS_AX + OWNER_AX)
    in_specs = (
        P(TOKENS_AX, None),
        P(TOKENS_AX, None),
        P(OWNER_AX, None, None, None),
        P(OWNER_AX, None, None, None),
        P(OWNER_AX, None),
        P(OWNER_AX, None),
        P(OWNER_AX),
    )
    out_specs = (
        P(TOKENS_AX, OWNER_AX),
        P(OWNER_AX, TOKENS_AX, None, None),
        P(OWNER_AX, TOKENS_AX, None, None),
    )
    return jax.shard_map(local, mesh=split, in_specs=in_specs, out_specs=out_specs, check_vma=False)
```

time: 762 us -> 107 us (0.14)
  the two profiles are of different devices: /device:TPU:2 before, /device:TPU:14 now
where the time goes in v1:
time: 107 us
  waiting for transfers between devices  32.9 us (31%)
  blocking collectives  21.9 us (20%)
  starting transfers between devices  19.7 us (18%)
  between operations  14.7 us (14%)
  Pallas kernels  8.8 us (8%)
  local copies, waits for them, and re-layouts  6.71 us (6%)
  other arithmetic  1.93 us (2%)
    all_to_all x1, blocking collectives, local(): lax.all_to_all(near.reshape(4, 6, tok, BLK), everyone, 0, 0, axis_index_g...  21.9 us
    all_to_all x1, waiting for transfers between devices, local(): lax.all_to_all(placed.reshape(4, 24, tok, BLK), everyone, 0, 0, axis_inde...  19.4 us
    all_to_all x1, starting transfers between devices, local(): far = lax.all_to_all(mid, ('ya', 'za'), 0, 0)  14.6 us
    all_to_all x1, waiting for transfers between devices, local(): far = lax.all_to_all(mid, ('ya', 'za'), 0, 0)  11.9 us
    pallas_call x1, Pallas kernels, local(): pl.pallas_call(layer_kernel, out_shape=(jax.ShapeDtypeStruct((N_Y * N_Z,...  8.8 us
    all_to_all x1, starting transfers between devices, local(): lax.all_to_all(placed.reshape(4, 24, tok, BLK), everyone, 0, 0, axis_inde...  5.11 us
    unnamed x9, local copies, waits for them, and re-layouts  4.99 us
  transfers between devices with their start and end apart: 3, of which 3 were waited for; matrix products, arithmetic and copies ran while one was open for 4% of the time, Pallas kernels for 0%

profile of v1, /device:TPU:14, one launch (start us, length us, event | category | flops | bytes accessed | tf_op | source)
XLA Modules:
  0.0 106.6 jit_solution(513223876228465366)
XLA Ops:
  7.8 0.0 copy-start
  7.8 1.4 %copy-done = bf16[2,24,128,128]{3,2,1,0:T(8,128)(2,1)S(1)} copy-done((bf16[2,24,128,128]{3,2,1,0:T(8,128)(2,1)S(1)}, bf16[2,24,128,128]{3,2,1,0:T(8,128)(2,1)}, u32[]{:S(2)}) %copy-start) | copy-done | bytes 1572888
  9.2 0.0 copy-start.1
  9.2 1.4 %copy-done.1 = bf16[2,24,128,128]{3,2,1,0:T(8,128)(2,1)S(1)} copy-done((bf16[2,24,128,128]{3,2,1,0:T(8,128)(2,1)S(1)}, bf16[2,24,128,128]{3,2,1,0:T(8,128)(2,1)}, u32[]{:S(2)}) %copy-start.1) | copy-done | bytes 1572888
  10.6 0.0 copy-start.2
  10.6 0.7 copy-done.2
  11.3 0.0 copy-start.3
  11.3 0.7 copy-done.3
  12.0 8.8 %shard_map.94 = (bf16[96,128,128]{2,1,0:T(8,128)(2,1)}, bf16[8,2,2,3,128,128]{5,4,3,2,1,0:T(8,128)(2,1)}) custom-call(s32[1]{0:T(128)} %bitcast.core, s32[2,24]{1,0:T(2,128)S(1)} %copy-done.2, s32[2,24]{1,0:T(2,128)S(1)} %copy-done.3, s32[1]{0:T(128)S(6)} %copy.11.count, bf16[128,12288]{1,0:T(8,128)(2,1)} %inputs.1, bf16[128,12288]{1,0:T(8,128)(2,1)} %out_grad.1, ...), custom_call_target="tpu_custom_call" | custom-call | tf_op jit(solution)/shard_map/pallas_call | solution.py:122
  20.8 5.1 %all-to-all-start = ((bf16[4,24,128,128]{3,2,1,0:T(8,128)(2,1)}), bf16[4,24,128,128]{3,2,1,0:T(8,128)(2,1)S(1)}, u32[]{:S(2)}, u32[]{:S(2)}) async-start(bf16[4,24,128,128]{3,2,1,0:T(8,128)(2,1)} %bitcast.17), calls=%async_computation | async-start | bytes 6291456 | tf_op jit(solution)/shard_map/all_to_all | solution.py:146
  25.9 0.0 reduce-scatter.2.cloned.1.call-start
  25.9 0.7 reduce-scatter.2.cloned.1.call-update
  26.6 19.4 %all-to-all-done = bf16[4,24,128,128]{3,2,1,0:T(8,128)(2,1)S(1)} async-done(((bf16[4,24,128,128]{3,2,1,0:T(8,128)(2,1)}), bf16[4,24,128,128]{3,2,1,0:T(8,128)(2,1)S(1)}, u32[]{:S(2)}, u32[]{:S(2)}) %all-to-all-start) | async-done | bytes 3145760 | tf_op jit(solution)/shard_map/all_to_all | solution.py:146
  46.0 0.5 add_convert_fusion
  46.5 21.9 %all_to_all.15 = bf16[4,6,128,128]{3,2,1,0:T(8,128)(2,1)S(1)} all-to-all(bf16[4,6,128,128]{3,2,1,0:T(8,128)(2,1)S(1)} %bitcast.18), channel_id=1, replica_groups={{0,2,24,26},{1,3,25,27},{4,6,28,30},{5,7,29,31},{8,10,32,34},{9,11,33,3..., dimensions={0} | all-to-all | bytes 1572864 | tf_op jit(solution)/shard_map/all_to_all | solution.py:150
  68.4 0.8 fusion
  69.2 14.6 %all-to-all-start.2 = ((bf16[6,128,128]{2,1,0:T(8,128)(2,1)}), bf16[6,128,128]{2,1,0:T(8,128)(2,1)S(1)}, u32[]{:S(2)}, u32[]{:S(2)}) async-start(bf16[6,128,128]{2,1,0:T(8,128)(2,1)} %fusion), calls=%async_computation.2 | async-start | bytes 393216 | tf_op jit(solution)/shard_map/all_to_all | solution.py:152
  83.8 0.9 reduce-scatter.2.cloned.1.call-done
  84.7 1.7 %slice_bitcast_fusion = (bf16[2,3,128,128]{3,2,1,0:T(8,128)(2,1)}, bf16[2,3,128,128]{2,3,1,0:T(8,128)(2,1)S(1)}) fusion(bf16[1,2,2,3,128,128]{5,4,3,2,1,0:T(8,128)(2,1)} %reduce-scatter.2.cloned.1.call-done), kind=kLoop, calls=%fused_computation.3 | loop fusion | bytes 786432 | tf_op jit(solution)/shard_map/squeeze | solution.py:143
  86.4 0.8 copy.10
  87.3 11.9 %all-to-all-done.2 = bf16[6,128,128]{2,1,0:T(8,128)(2,1)S(1)} async-done(((bf16[6,128,128]{2,1,0:T(8,128)(2,1)}), bf16[6,128,128]{2,1,0:T(8,128)(2,1)S(1)}, u32[]{:S(2)}, u32[]{:S(2)}) %all-to-all-start.2) | async-done | bytes 196640 | tf_op jit(solution)/shard_map/all_to_all | solution.py:152
  99.1 0.6 fusion.1
Async XLA Ops:
  7.8 1.4 %copy-start = (bf16[2,24,128,128]{3,2,1,0:T(8,128)(2,1)S(1)}, bf16[2,24,128,128]{3,2,1,0:T(8,128)(2,1)}, u32[]{:S(2)}) copy-start(bf16[2,24,128,128]{3,2,1,0:T(8,128)(2,1)} %param.9) | copy-start | bytes 4718596
  9.2 1.4 %copy-start.1 = (bf16[2,24,128,128]{3,2,1,0:T(8,128)(2,1)S(1)}, bf16[2,24,128,128]{3,2,1,0:T(8,128)(2,1)}, u32[]{:S(2)}) copy-start(bf16[2,24,128,128]{3,2,1,0:T(8,128)(2,1)} %param.10) | copy-start | bytes 4718596
  10.6 0.7 copy-start.2
  11.3 0.7 copy-start.3
  20.8 25.2 %all-to-all-start = ((bf16[4,24,128,128]{3,2,1,0:T(8,128)(2,1)}), bf16[4,24,128,128]{3,2,1,0:T(8,128)(2,1)S(1)}, u32[]{:S(2)}, u32[]{:S(2)}) async-start(bf16[4,24,128,128]{3,2,1,0:T(8,128)(2,1)} %bitcast.17), calls=%async_computation | async-start | bytes 6291456 | tf_op jit(solution)/shard_map/all_to_all | solution.py:146
  25.9 58.8 %reduce-scatter.2.cloned.1.call-start = ((), (), s32[]{:S(2)}) async-start(), calls=%async_computation.4 | async-start | bytes 3538944 | tf_op jit(solution)/shard_map/reduce_scatter | solution.py:141
  69.2 30.0 %all-to-all-start.2 = ((bf16[6,128,128]{2,1,0:T(8,128)(2,1)}), bf16[6,128,128]{2,1,0:T(8,128)(2,1)S(1)}, u32[]{:S(2)}, u32[]{:S(2)}) async-start(bf16[6,128,128]{2,1,0:T(8,128)(2,1)} %fusion), calls=%async_computation.2 | async-start | bytes 393216 | tf_op jit(solution)/shard_map/all_to_all | solution.py:152
Sparse Core Ops, SparseCore 0:
  29.9 54.8 reduce-scatter.1

commit v2 on v1

v2 whole, which is shorter than its diff:
```python
import jax
import jax.numpy as jnp
from jax import lax
from jax.experimental import pallas as pl
from jax.experimental.pallas import tpu as pltpu
from jax.sharding import Mesh
from jax.sharding import PartitionSpec as P

BLK = 128
VMEM_LIMIT = 60 * 1024 * 1024
N_DP, N_SEQ, N_Y, N_Z = 2, 4, 8, 12
TOKENS_AX = ("dp", "seq")
OWNER_AX = ("y", "z")


def gelu_pair(pre_act):
    squared = pre_act * pre_act
    tangent = jnp.tanh(0.7978845608 * (pre_act + 0.044715 * squared * pre_act))
    value = 0.5 * pre_act * (1.0 + tangent)
    slope = 0.5 * (1.0 + tangent) + 0.5 * pre_act * (1.0 - tangent * tangent) * 0.7978845608 * (
        1.0 + 3.0 * 0.044715 * squared
    )
    return value, slope


def two_blocks(ref, first, second):
    return jnp.concatenate(
        [
            ref[:, pl.ds(pl.multiple_of(first * BLK, BLK), BLK)],
            ref[:, pl.ds(pl.multiple_of(second * BLK, BLK), BLK)],
        ],
        axis=1,
    )


def fetch_columns(source, indices, target, sem):
    for i, index in enumerate(indices):
        columns = source.at[:, pl.ds(pl.multiple_of(index * BLK, BLK), BLK)]
        pltpu.make_async_copy(columns, target.at[i], sem).start()


def wait_for(target, sem):
    pltpu.make_async_copy(target, target, sem).wait()


def dot_nn(left, right):
    return lax.dot_general(left, right, (((1,), (0,)), ((), ())), preferred_element_type=jnp.float32)


def dot_nt(left, right):
    return lax.dot_general(left, right, (((1,), (1,)), ((), ())), preferred_element_type=jnp.float32)


def ring_place(size, far_groups):
    first = [0 if p % 4 in (0, 3) else 1 for p in range(size)]
    third = {p: group.index(p) for group in far_groups for p in group}
    second = {}
    for group in far_groups:
        for p in group:
            second[p] = 0 if min(group) in (0, 1) else 1
    return [(first[p], second[p], third[p]) for p in range(size)]


FAR_Y = [[0, 3], [1, 6], [2, 5], [4, 7]]
FAR_Z = [[p, p + 4, p + 8] for p in range(4)]
PLACE_Y, PLACE_Z = ring_place(N_Y, FAR_Y), ring_place(N_Z, FAR_Z)


def place_table():
    table = []
    for core in range(N_DP):
        for r in range(N_Y * N_Z):
            a, b = PLACE_Y[(r // N_Z - core) % N_Y], PLACE_Z[(r % N_Z - core) % N_Z]
            table.append(((a[0] * 2 + b[0]) * 4 + a[1] * 2 + b[1]) * 6 + a[2] * 3 + b[2])
    return table


def owner_groups(groups_y, groups_z):
    return [
        [
            ((core * N_SEQ + seq) * N_Y + (y + core) % N_Y) * N_Z + (z + core) % N_Z
            for y in group_y
            for z in group_z
        ]
        for core in range(N_DP)
        for seq in range(N_SEQ)
        for group_y in groups_y
        for group_z in groups_z
    ]


def neighbours(size, start, step):
    place = PLACE_Y if size == N_Y else PLACE_Z
    return [sorted((p, (p + 1) % size), key=lambda q: place[q][step]) for p in range(start, size, 2)]


def forward_kernel(
    core, place_hbm, rows_hbm, cols_hbm, count_hbm, inputs_hbm, out_grad_hbm, ups_hbm, downs_hbm,
    placed_hbm, hidden_t, pre_grad_t,
    placed, inputs, out_grad, ups, downs, place, rows, cols, count, small_sems, sems, out_sem,
):
    slots, fan = rows.shape
    tok = inputs.shape[0]
    small = [
        pltpu.make_async_copy(source, target, small_sems.at[i])
        for i, (source, target) in enumerate(
            ((rows_hbm, rows), (cols_hbm, cols), (place_hbm, place), (count_hbm, count))
        )
    ]
    large = [
        pltpu.make_async_copy(source, target, sems.at[i])
        for i, (source, target) in enumerate(
            (
                (ups_hbm.at[0], ups.at[0]),
                (inputs_hbm, inputs),
                (downs_hbm.at[0], downs.at[0]),
                (out_grad_hbm, out_grad),
                (ups_hbm.at[1], ups.at[1]),
                (downs_hbm.at[1], downs.at[1]),
            )
        )
    ]
    for copy in small + large:
        copy.start()
    placed[...] = jnp.zeros_like(placed)
    for copy in small:
        copy.wait()
    for s in range(slots):
        live = (s < count[0]).astype(jnp.float32)
        for copy in large[:2] if s == 0 else large[4:5]:
            copy.wait()
        pre_act = jnp.zeros((tok, BLK), jnp.float32)
        for k in range(0, fan, 2):
            pre_act += dot_nn(
                two_blocks(inputs, rows[s, k], rows[s, k + 1]), ups[s, k * BLK : (k + 2) * BLK, :]
            )
        for copy in large[2:4] if s == 0 else large[5:]:
            copy.wait()
        hid_grad = jnp.zeros((tok, BLK), jnp.float32)
        for k in range(0, fan, 2):
            hid_grad += dot_nt(
                two_blocks(out_grad, cols[s, k], cols[s, k + 1]),
                jnp.concatenate([downs[s, k * BLK : (k + 1) * BLK, :], downs[s, (k + 1) * BLK : (k + 2) * BLK, :]], axis=1),
            )
        value, slope = gelu_pair(pre_act)
        hidden_t[s] = jnp.transpose(value * live).astype(jnp.bfloat16)
        turned = jnp.transpose(hid_grad * slope * live).astype(jnp.bfloat16)
        pre_grad_t[s] = turned
        for k in range(0, fan, 2):
            both = dot_nn(ups[s, k * BLK : (k + 2) * BLK, :], turned)
            for i in range(2):
                at = place[core[0], rows[s, k + i]]
                product = both[i * BLK : (i + 1) * BLK, :]
                if s > 0:
                    product += placed[at].astype(jnp.float32)
                placed[at] = product.astype(jnp.bfloat16)
    write = pltpu.make_async_copy(placed, placed_hbm, out_sem)
    write.start()
    write.wait()


def weight_kernel(
    core, seq, rows, cols, inputs, out_grad,
    hidden_t, pre_grad_t, theirs_far, theirs_near, mine_far, mine_near, fetched, sems,
):
    slots = rows.shape[0]
    parts, each = mine_far.shape[0], mine_far.shape[3]
    here, there = core[0] * N_SEQ, (1 - core[0]) * N_SEQ
    flip, mirror, across = seq[0] ^ 1, 3 - seq[0], seq[0] ^ 2
    first = jnp.where(core[0] == 0, flip, mirror)
    second = flip + mirror - first
    targets = (
        (theirs_far, (there + second, there + across)),
        (theirs_near, (there + seq[0], there + first)),
        (mine_far, (here + first, here + across)),
        (mine_near, (here + seq[0], here + second)),
    )
    for half, (data, ids) in enumerate(((inputs, rows), (out_grad, cols))):
        for t, (_, groups) in enumerate(targets):
            for s in range(slots):
                ks = [group * each + i for group in groups for i in range(each)]
                fetch_columns(data, [ids[s, k] for k in ks], fetched.at[half, t, s], sems.at[half, t])
    for half, left in enumerate((pre_grad_t, hidden_t)):
        for t, (target, _) in enumerate(targets):
            wait_for(fetched.at[half, t], sems.at[half, t])
            for s in range(slots):
                for j in range(0, parts * each, 2):
                    pair = jnp.concatenate([fetched[half, t, s, j], fetched[half, t, s, j + 1]], axis=1)
                    both = dot_nn(left[s], pair)
                    for i in range(2):
                        value = both[:, i * BLK : (i + 1) * BLK]
                        target[(j + i) // each, half, s, (j + i) % each] = value.astype(jnp.bfloat16)


def small_call(kernel, out_shape, *operands):
    vmem = pl.BlockSpec(memory_space=pltpu.VMEM)
    return pl.pallas_call(
        kernel,
        out_shape=out_shape,
        in_specs=[vmem] * len(operands),
        out_specs=jax.tree.map(lambda _: vmem, out_shape),
        compiler_params=pltpu.CompilerParams(vmem_limit_bytes=8 * 1024 * 1024),
    )(*operands)


def sum_first_kernel(terms, total):
    value = terms[0].astype(jnp.float32)
    for i in range(1, terms.shape[0]):
        value += terms[i].astype(jnp.float32)
    total[...] = value.astype(jnp.bfloat16)


def sum_first(terms):
    return small_call(sum_first_kernel, jax.ShapeDtypeStruct(terms.shape[1:], terms.dtype), terms)


def sum_large_kernel(terms_hbm, total, terms, sems):
    steps = sems.shape[0]
    rows = total.shape[0] // steps
    pieces = [pl.ds(i * rows, rows) for i in range(steps)]
    copies = [
        pltpu.make_async_copy(terms_hbm.at[:, piece], terms.at[:, piece], sems.at[i])
        for i, piece in enumerate(pieces)
    ]
    for copy in copies:
        copy.start()
    for copy, piece in zip(copies, pieces):
        copy.wait()
        value = terms[0, piece].astype(jnp.float32)
        for i in range(1, terms.shape[0]):
            value += terms[i, piece].astype(jnp.float32)
        total[piece] = value.astype(jnp.bfloat16)


def sum_large(terms):
    return pl.pallas_call(
        sum_large_kernel,
        out_shape=jax.ShapeDtypeStruct(terms.shape[1:], terms.dtype),
        in_specs=[pl.BlockSpec(memory_space=pltpu.HBM)],
        out_specs=pl.BlockSpec(memory_space=pltpu.VMEM),
        scratch_shapes=[pltpu.VMEM(terms.shape, terms.dtype), pltpu.SemaphoreType.DMA((6,))],
        compiler_params=pltpu.CompilerParams(vmem_limit_bytes=VMEM_LIMIT),
    )(terms)


def add_kernel(*refs):
    *terms, total = refs
    last = total.shape[0]
    value = sum(term[term.shape[0] - last :].astype(jnp.float32) for term in terms)
    total[...] = value.astype(jnp.bfloat16)


def add_last(count, *terms):
    return small_call(add_kernel, jax.ShapeDtypeStruct((count,) + terms[0].shape[1:], terms[0].dtype), *terms)


def weight_end_kernel(*refs):
    *terms, up_grad, down_grad = refs
    slots, each = up_grad.shape[:2]
    for s in range(slots):
        for i in range(each):
            up = sum(term[0, 0, s, i].astype(jnp.float32) for term in terms)
            down = sum(term[0, 1, s, i].astype(jnp.float32) for term in terms)
            up_grad[s, i] = jnp.transpose(up).astype(jnp.bfloat16)
            down_grad[s, i] = down.astype(jnp.bfloat16)


def input_end_kernel(terms, input_grad):
    total = terms[0].astype(jnp.float32)
    for i in range(1, terms.shape[0]):
        total += terms[i].astype(jnp.float32)
    input_grad[...] = jnp.transpose(total).astype(jnp.bfloat16)


def core_seq_pairs(partner):
    return [
        (core * N_SEQ + seq, core * N_SEQ + partner(core, seq)) for core in range(N_DP) for seq in range(N_SEQ)
    ]


def local(inputs, out_grad, up_blocks, down_blocks, up_rows, down_cols, slot_count):
    tok, features = inputs.shape
    slots, fan = up_rows.shape
    each = fan // (N_DP * N_SEQ)
    bf16 = jnp.bfloat16
    smem = pl.BlockSpec(memory_space=pltpu.SMEM)
    vmem = pl.BlockSpec(memory_space=pltpu.VMEM)
    hbm = pl.BlockSpec(memory_space=pltpu.HBM)
    core = lax.axis_index("dp").astype(jnp.int32)
    seq = lax.axis_index("seq").astype(jnp.int32)
    wide = (slots, fan * BLK, BLK)
    placed, hidden_t, pre_grad_t = pl.pallas_call(
        forward_kernel,
        out_shape=(
            jax.ShapeDtypeStruct((N_Y * N_Z, BLK, tok), bf16),
            jax.ShapeDtypeStruct((slots, BLK, tok), bf16),
            jax.ShapeDtypeStruct((slots, BLK, tok), bf16),
        ),
        in_specs=[smem] + [hbm] * 8,
        out_specs=(hbm, vmem, vmem),
        scratch_shapes=[
            pltpu.VMEM((N_Y * N_Z, BLK, tok), bf16),
            pltpu.VMEM((tok, features), bf16),
            pltpu.VMEM((tok, features), bf16),
            pltpu.VMEM(wide, bf16),
            pltpu.VMEM(wide, bf16),
            pltpu.SMEM((N_DP, N_Y * N_Z), jnp.int32),
            pltpu.SMEM((slots, fan), jnp.int32),
            pltpu.SMEM((slots, fan), jnp.int32),
            pltpu.SMEM((1,), jnp.int32),
            pltpu.SemaphoreType.DMA((4,)),
            pltpu.SemaphoreType.DMA((6,)),
            pltpu.SemaphoreType.DMA(()),
        ],
        compiler_params=pltpu.CompilerParams(vmem_limit_bytes=VMEM_LIMIT),
    )(
        core.reshape(1),
        jnp.asarray(place_table(), jnp.int32).reshape(N_DP, N_Y * N_Z),
        up_rows,
        down_cols,
        slot_count,
        inputs,
        out_grad,
        up_blocks.reshape(wide),
        down_blocks.reshape(wide),
    )
    everyone = TOKENS_AX + OWNER_AX
    near = lax.all_to_all(
        placed.reshape(4, 24, BLK, tok), everyone, 0, 0, axis_index_groups=owner_groups(neighbours(N_Y, 0, 0), neighbours(N_Z, 0, 0))
    )

    part_shape = jax.ShapeDtypeStruct((2, 2, slots, each, BLK, BLK), bf16)
    theirs_far, theirs_near, mine_far, mine_near = pl.pallas_call(
        weight_kernel,
        out_shape=(part_shape,) * 4,
        in_specs=[smem] * 4 + [hbm] * 2 + [vmem] * 2,
        out_specs=(vmem,) * 4,
        scratch_shapes=[
            pltpu.VMEM((2, 4, slots, 2 * each, tok, BLK), bf16),
            pltpu.SemaphoreType.DMA((2, 4)),
        ],
        compiler_params=pltpu.CompilerParams(vmem_limit_bytes=12 * 1024 * 1024),
        cost_estimate=pl.CostEstimate(flops=400_000_000, bytes_accessed=10_000_000, transcendentals=0),
    )(core.reshape(1), seq.reshape(1), up_rows, down_cols, inputs, out_grad, hidden_t, pre_grad_t)
    other_core = [(0, 1), (1, 0)]
    far_arrived = lax.ppermute(theirs_far, "dp", other_core)
    near_arrived = lax.ppermute(theirs_near, "dp", other_core)
    first_got = lax.ppermute(
        add_last(2, mine_far, far_arrived), TOKENS_AX, core_seq_pairs(lambda c, q: 3 - q if c else q ^ 1)
    )
    near, _, _ = lax.optimization_barrier((near, far_arrived, near_arrived))
    mid = lax.all_to_all(
        sum_large(near).reshape(4, 6, BLK, tok),
        everyone,
        0,
        0,
        axis_index_groups=owner_groups(neighbours(N_Y, 1, 1), neighbours(N_Z, 1, 1)),
    )
    second_got = lax.ppermute(
        add_last(1, mine_near, near_arrived, first_got),
        TOKENS_AX,
        core_seq_pairs(lambda c, q: q ^ 1 if c else 3 - q),
    )
    far = lax.all_to_all(sum_first(mid), everyone, 0, 0, axis_index_groups=owner_groups(FAR_Y, FAR_Z))

    grad_shape = jax.ShapeDtypeStruct((slots, each, BLK, BLK), bf16)
    up_grad, down_grad = small_call(
        weight_end_kernel, (grad_shape, grad_shape), mine_near, near_arrived, first_got, second_got
    )
    input_grad = small_call(input_end_kernel, jax.ShapeDtypeStruct((tok, BLK), bf16), far)
    return input_grad, up_grad, down_grad


def solution(mesh):
    split = Mesh(mesh.devices.reshape(N_DP, N_SEQ, N_Y, N_Z), TOKENS_AX + OWNER_AX)
    in_specs = (
        P(TOKENS_AX, None),
        P(TOKENS_AX, None),
        P(OWNER_AX, None, None, None),
        P(OWNER_AX, None, None, None),
        P(OWNER_AX, None),
        P(OWNER_AX, None),
        P(OWNER_AX),
    )
    out_specs = (
        P(TOKENS_AX, OWNER_AX),
        P(OWNER_AX, TOKENS_AX, None, None),
        P(OWNER_AX, TOKENS_AX, None, None),
    )
    return jax.shard_map(local, mesh=split, in_specs=in_specs, out_specs=out_specs, check_vma=False)
```

time: 107 us -> 86.1 us (0.80)
  the two profiles are of different devices: /device:TPU:14 before, /device:TPU:20 now
where the time goes in v2:
time: 86.1 us; the launch traced here: 85.5 us
  starting transfers between devices  44 us (51%)
  Pallas kernels  18.8 us (22%)
  waiting for transfers between devices  15.5 us (18%)
  local copies, waits for them, and re-layouts  5.77 us (7%)
  between operations  1.45 us (2%)
    all_to_all x1, starting transfers between devices, local(): lax.all_to_all(sum_large(near).reshape(4, 6, BLK, tok), everyone, 0, 0, a...  13.5 us
    ppermute x1, starting transfers between devices, local(): far_arrived = lax.ppermute(theirs_far, 'dp', other_core)  10.5 us
    pallas_call x1, Pallas kernels, local(): pl.pallas_call(forward_kernel, out_shape=(jax.ShapeDtypeStruct((N_Y * N_Z...  8.46 us
    ppermute x1, waiting for transfers between devices, local(): lax.ppermute(add_last(1, mine_near, near_arrived, first_got), TOKENS_AX,...  7.22 us
    all_to_all x1, starting transfers between devices, local(): lax.all_to_all(placed.reshape(4, 24, BLK, tok), everyone, 0, 0, axis_inde...  6.45 us
    all_to_all x1, starting transfers between devices, local(): lax.all_to_all(sum_first(mid), everyone, 0, 0, axis_index_groups=owner_gr...  6.12 us
    unnamed x24, local copies, waits for them, and re-layouts  5.77 us
    pallas_call x1, Pallas kernels, local(): pl.pallas_call(weight_kernel, out_shape=(part_shape,) * 4, in_specs=[smem...  3.84 us
  transfers between devices with their start and end apart: 7, of which 5 were waited for; matrix products, arithmetic and copies ran while one was open for 0% of the time, Pallas kernels for 8%

profile of v2, /device:TPU:20, one launch (start us, length us, event | category | flops | bytes accessed | tf_op | source)
XLA Modules:
  0.0 85.5 jit_solution(1354676095084211622)
XLA Ops:
  1.3 8.5 %shard_map.103 = (bf16[96,128,128]{2,1,0:T(8,128)(2,1)}, bf16[2,128,128]{2,1,0:T(8,128)(2,1)}, bf16[2,128,128]{2,1,0:T(8,128)(2,1)}) custom-call(s32[1]{0:T(128)} %bitcast.core, s32[2,96]{1,0:T(2,128)} %constant.18.place_hbm, s32[2,24]{1,0:T(2,128)} %rows.1, s32[2,24]{1,0:T(2,128)} %cols.1, s32[1]{0:T(128)S(6)} %copy.11.count_hbm, ...), custom_call_target="tpu_custom_call" | custom-call | tf_op jit(solution)/shard_map/pallas_call | solution.py:292
  9.8 0.0 copy-start
  9.8 0.0 copy-start.8
  9.8 0.0 copy-start.9
  9.8 0.0 copy-start.10
  9.8 0.0 copy-start.11
  9.8 6.5 %all-to-all-start = ((bf16[4,24,128,128]{3,2,1,0:T(8,128)(2,1)}), bf16[4,24,128,128]{3,2,1,0:T(8,128)(2,1)}, u32[]{:S(2)}, u32[]{:S(2)}) async-start(bf16[4,24,128,128]{3,2,1,0:T(8,128)(2,1)} %bitcast.6), calls=%async_computation | async-start | bytes 6291456 | tf_op jit(solution)/shard_map/all_to_all | solution.py:328
  16.3 0.0 copy-start.1
  16.3 1.9 %copy-done.1 = bf16[128,12288]{1,0:T(8,128)(2,1)S(1)} copy-done((bf16[128,12288]{1,0:T(8,128)(2,1)S(1)}, bf16[128,12288]{1,0:T(8,128)(2,1)}, u32[]{:S(2)}) %copy-start.1) | copy-done | bytes 3145752
  18.2 3.8 %shard_map.104 = (bf16[2,2,2,3,128,128]{5,4,3,2,1,0:T(8,128)(2,1)S(1)}, bf16[2,2,2,3,128,128]{5,4,3,2,1,0:T(8,128)(2,1)S(1)}, bf16[2,2,2,3,128,128]{5,4,3,2,1,0:...) custom-call(s32[1]{0:T(128)} %bitcast.core, s32[1]{0:T(128)} %bitcast.4.seq, s32[2,24]{1,0:T(2,128)S(1)} %copy-done.10, ...), custom_call_target="tpu_custom_call" | custom-call | flops 400000000 | bytes 10000000 | tf_op jit(solution)/shard_map/pallas_call | solution.py:333
  22.0 0.9 %copy-done.2 = bf16[2,2,2,3,128,128]{5,4,3,2,1,0:T(8,128)(2,1)} copy-done((bf16[2,2,2,3,128,128]{5,4,3,2,1,0:T(8,128)(2,1)}, bf16[2,2,2,3,128,128]{5,4,3,2,1,0:T(8,128)(2,1)S(1)}, u32[]{:S(2)}) %copy-start.2) | copy-done | bytes 786456
  22.9 0.9 %copy-done.4 = bf16[2,2,2,3,128,128]{5,4,3,2,1,0:T(8,128)(2,1)} copy-done((bf16[2,2,2,3,128,128]{5,4,3,2,1,0:T(8,128)(2,1)}, bf16[2,2,2,3,128,128]{5,4,3,2,1,0:T(8,128)(2,1)S(1)}, u32[]{:S(2)}) %copy-start.4) | copy-done | bytes 786456
  23.8 10.5 %collective-permute-start = (bf16[2,2,2,3,128,128]{5,4,3,2,1,0:T(8,128)(2,1)S(1)}, bf16[2,2,2,3,128,128]{5,4,3,2,1,0:T(8,128)(2,1)S(1)}, u32[]{:S(2)}, u32[]{:S(2)}) collective-permute-start(bf16[2,2,2,3,128,128]{5,4,3,2,1,0:T(8,128)(2,1)S(1)} %get-tuple-element.16), channel_id=1, source_target_pairs={{0,384},{384,0},{1,385},{385,1},{2,386},{386,2},{3,387},{387,3},{4... | collective-permute-start | bytes 2359304 | tf_op jit(solution)/shard_map/ppermute | solution.py:346
  34.4 1.9 %collective-permute-start.1 = (bf16[2,2,2,3,128,128]{5,4,3,2,1,0:T(8,128)(2,1)S(1)}, bf16[2,2,2,3,128,128]{5,4,3,2,1,0:T(8,128)(2,1)S(1)}, u32[]{:S(2)}, u32[]{:S(2)}) collective-permute-start(bf16[2,2,2,3,128,128]{5,4,3,2,1,0:T(8,128)(2,1)S(1)} %get-tuple-element.17), channel_id=1, source_target_pairs={{0,384},{384,0},{1,385},{385,1},{2,386},{386,2},{3,387},{387,3},{4... | collective-permute-start | bytes 2359304 | tf_op jit(solution)/shard_map/ppermute | solution.py:347
  36.3 0.0 collective-permute-done.refs_1_
  36.3 0.9 %copy-done.6 = bf16[2,2,2,3,128,128]{5,4,3,2,1,0:T(8,128)(2,1)} copy-done((bf16[2,2,2,3,128,128]{5,4,3,2,1,0:T(8,128)(2,1)}, bf16[2,2,2,3,128,128]{5,4,3,2,1,0:T(8,128)(2,1)S(1)}, u32[]{:S(2)}) %copy-start.6) | copy-done | bytes 786456
  37.2 1.3 %collective-permute-done.1.refs_1_ = bf16[2,2,2,3,128,128]{5,4,3,2,1,0:T(8,128)(2,1)S(1)} collective-permute-done((bf16[2,2,2,3,128,128]{5,4,3,2,1,0:T(8,128)(2,1)S(1)}, bf16[2,2,2,3,128,128]{5,4,3,2,1,0:T(8,128)(2,1)S(1)}, u32[]{:S(2)}, u32[]{:S(2)}) %collective-permute-start.1) | collective-permute-done | bytes 786464 | tf_op jit(solution)/shard_map/ppermute | solution.py:347
  38.5 2.8 %shard_map.105 = bf16[24,128,128]{2,1,0:T(8,128)(2,1)} custom-call(bf16[4,24,128,128]{3,2,1,0:T(8,128)(2,1)} %all-to-all-done.terms_hbm), custom_call_target="tpu_custom_call" | custom-call | tf_op jit(solution)/shard_map/pallas_call | solution.py:236
  41.4 13.5 %all-to-all-start.1 = ((bf16[4,6,128,128]{3,2,1,0:T(8,128)(2,1)}), bf16[4,6,128,128]{3,2,1,0:T(8,128)(2,1)S(1)}, u32[]{:S(2)}, u32[]{:S(2)}) async-start(bf16[4,6,128,128]{3,2,1,0:T(8,128)(2,1)} %bitcast.7), calls=%async_computation.1 | async-start | bytes 1572864 | tf_op jit(solution)/shard_map/all_to_all | solution.py:352
  54.9 1.1 %copy-done.7 = bf16[2,2,2,3,128,128]{5,4,3,2,1,0:T(8,128)(2,1)S(1)} copy-done((bf16[2,2,2,3,128,128]{5,4,3,2,1,0:T(8,128)(2,1)S(1)}, bf16[2,2,2,3,128,128]{5,4,3,2,1,0:T(8,128)(2,1)}, u32[]{:S(2)}) %copy-start.7) | copy-done | bytes 786456
  56.0 1.1 %shard_map.108 = bf16[2,2,2,3,128,128]{5,4,3,2,1,0:T(8,128)(2,1)} custom-call(bf16[2,2,2,3,128,128]{5,4,3,2,1,0:T(8,128)(2,1)S(1)} %copy-done.5, bf16[2,2,2,3,128,128]{5,4,3,2,1,0:T(8,128)(2,1)S(1)} %copy-done.7), custom_call_target="tpu_custom_call" | custom-call | tf_op jit(solution)/shard_map/pallas_call | solution.py:197
  57.1 3.1 %collective-permute-start.2 = (bf16[2,2,2,3,128,128]{5,4,3,2,1,0:T(8,128)(2,1)}, bf16[2,2,2,3,128,128]{5,4,3,2,1,0:T(8,128)(2,1)S(1)}, u32[]{:S(2)}, u32[]{:S(2)}) collective-permute-start(bf16[2,2,2,3,128,128]{5,4,3,2,1,0:T(8,128)(2,1)} %shard_map.108), channel_id=1, source_target_pairs={{0,96},{96,0},{192,288},{288,192},{384,672},{480,576},{576,480},{6... | collective-permute-start | bytes 2359304 | tf_op jit(solution)/shard_map/ppermute | solution.py:348
  60.2 3.3 %all-to-all-done.1.terms = bf16[4,6,128,128]{3,2,1,0:T(8,128)(2,1)S(1)} async-done(((bf16[4,6,128,128]{3,2,1,0:T(8,128)(2,1)}), bf16[4,6,128,128]{3,2,1,0:T(8,128)(2,1)S(1)}, u32[]{:S(2)}, u32[]{:S(2)}) %all-to-all-start.1) | async-done | bytes 786464 | tf_op jit(solution)/shard_map/all_to_all | solution.py:352
  63.5 0.8 shard_map.106
  64.3 6.1 %all-to-all-start.2 = ((bf16[6,128,128]{2,1,0:T(8,128)(2,1)}), bf16[6,128,128]{2,1,0:T(8,128)(2,1)S(1)}, u32[]{:S(2)}, u32[]{:S(2)}) async-start(bf16[6,128,128]{2,1,0:T(8,128)(2,1)} %shard_map.106), calls=%async_computation.2 | async-start | bytes 393216 | tf_op jit(solution)/shard_map/all_to_all | solution.py:364
  70.4 0.7 collective-permute-done.2.refs_2_
  71.2 0.1 shard_map.109
  71.3 2.4 %collective-permute-start.3 = (bf16[1,2,2,3,128,128]{5,4,3,2,1,0:T(8,128)(2,1)S(1)}, bf16[1,2,2,3,128,128]{5,4,3,2,1,0:T(8,128)(2,1)S(1)}, u32[]{:S(2)}, u32[]{:S(2)}) collective-permute-start(bf16[1,2,2,3,128,128]{5,4,3,2,1,0:T(8,128)(2,1)S(1)} %shard_map.109), channel_id=1, source_target_pairs={{0,288},{96,192},{192,96},{288,0},{384,480},{480,384},{576,672},{6... | collective-permute-start | bytes 1179656 | tf_op jit(solution)/shard_map/ppermute | solution.py:359
  73.8 7.2 %collective-permute-done.3.refs_3_ = bf16[1,2,2,3,128,128]{5,4,3,2,1,0:T(8,128)(2,1)S(1)} collective-permute-done((bf16[1,2,2,3,128,128]{5,4,3,2,1,0:T(8,128)(2,1)S(1)}, bf16[1,2,2,3,128,128]{5,4,3,2,1,0:T(8,128)(2,1)S(1)}, u32[]{:S(2)}, u32[]{:S(2)}) %collective-permute-start.3) | collective-permute-done | bytes 393248 | tf_op jit(solution)/shard_map/ppermute | solution.py:359
  81.0 0.9 %shard_map.110 = (bf16[2,3,128,128]{3,2,1,0:T(8,128)(2,1)}, bf16[2,3,128,128]{3,2,1,0:T(8,128)(2,1)}) custom-call(bf16[2,2,2,3,128,128]{5,4,3,2,1,0:T(8,128)(2,1)S(1)} %copy-done.3, bf16[2,2,2,3,128,128]{5,4,3,2,1,0:T(8,128)(2,1)S(1)} %collective-permute-done.1.refs_1_, bf16[2,2,2,3,128,128]{5,4,3,2,1,0:T(8,128)(2,1)S(1)} %collective-permute-done.2.refs_2_, ...), custom_call_target="tpu_custom_call" | custom-call | tf_op jit(solution)/shard_map/pallas_call | solution.py:197
  81.9 2.9 %all-to-all-done.2.terms = bf16[6,128,128]{2,1,0:T(8,128)(2,1)S(1)} async-done(((bf16[6,128,128]{2,1,0:T(8,128)(2,1)}), bf16[6,128,128]{2,1,0:T(8,128)(2,1)S(1)}, u32[]{:S(2)}, u32[]{:S(2)}) %all-to-all-start.2) | async-done | bytes 196640 | tf_op jit(solution)/shard_map/all_to_all | solution.py:364
  84.8 0.7 shard_map.107
  (14 shorter events, 0.0 us)
Async XLA Ops:
  9.8 6.5 %copy-start = (bf16[128,12288]{1,0:T(8,128)(2,1)S(1)}, bf16[128,12288]{1,0:T(8,128)(2,1)}, u32[]{:S(2)}) copy-start(bf16[128,12288]{1,0:T(8,128)(2,1)} %inputs.1) | copy-start | bytes 9437188
  9.8 6.5 %copy-start.8 = (bf16[2,128,128]{2,1,0:T(8,128)(2,1)S(1)}, bf16[2,128,128]{2,1,0:T(8,128)(2,1)}, u32[]{:S(2)}) copy-start(bf16[2,128,128]{2,1,0:T(8,128)(2,1)} %get-tuple-element.14.hidden_t) | copy-start | bytes 196612
  9.8 6.5 %copy-start.9 = (bf16[2,128,128]{2,1,0:T(8,128)(2,1)S(1)}, bf16[2,128,128]{2,1,0:T(8,128)(2,1)}, u32[]{:S(2)}) copy-start(bf16[2,128,128]{2,1,0:T(8,128)(2,1)} %get-tuple-element.15.pre_grad_t) | copy-start | bytes 196612
  9.8 6.5 %copy-start.10 = (s32[2,24]{1,0:T(2,128)S(1)}, s32[2,24]{1,0:T(2,128)}, u32[]{:S(2)}) copy-start(s32[2,24]{1,0:T(2,128)} %rows.1) | copy-start | bytes 580
  9.8 6.5 %copy-start.11 = (s32[2,24]{1,0:T(2,128)S(1)}, s32[2,24]{1,0:T(2,128)}, u32[]{:S(2)}) copy-start(s32[2,24]{1,0:T(2,128)} %cols.1) | copy-start | bytes 580
  9.8 28.7 %all-to-all-start = ((bf16[4,24,128,128]{3,2,1,0:T(8,128)(2,1)}), bf16[4,24,128,128]{3,2,1,0:T(8,128)(2,1)}, u32[]{:S(2)}, u32[]{:S(2)}) async-start(bf16[4,24,128,128]{3,2,1,0:T(8,128)(2,1)} %bitcast.6), calls=%async_computation | async-start | bytes 6291456 | tf_op jit(solution)/shard_map/all_to_all | solution.py:328
  16.3 1.9 %copy-start.1 = (bf16[128,12288]{1,0:T(8,128)(2,1)S(1)}, bf16[128,12288]{1,0:T(8,128)(2,1)}, u32[]{:S(2)}) copy-start(bf16[128,12288]{1,0:T(8,128)(2,1)} %out_grad.1) | copy-start | bytes 9437188
  22.0 0.9 %copy-start.2 = (bf16[2,2,2,3,128,128]{5,4,3,2,1,0:T(8,128)(2,1)}, bf16[2,2,2,3,128,128]{5,4,3,2,1,0:T(8,128)(2,1)S(1)}, u32[]{:S(2)}) copy-start(bf16[2,2,2,3,128,128]{5,4,3,2,1,0:T(8,128)(2,1)S(1)} %get-tuple-element.19.refs_0_) | copy-start | bytes 2359300
  22.9 0.9 %copy-start.4 = (bf16[2,2,2,3,128,128]{5,4,3,2,1,0:T(8,128)(2,1)}, bf16[2,2,2,3,128,128]{5,4,3,2,1,0:T(8,128)(2,1)S(1)}, u32[]{:S(2)}) copy-start(bf16[2,2,2,3,128,128]{5,4,3,2,1,0:T(8,128)(2,1)S(1)} %get-tuple-element.20.refs_0_) | copy-start | bytes 2359300
  23.8 31.1 %copy-start.5 = (bf16[2,2,2,3,128,128]{5,4,3,2,1,0:T(8,128)(2,1)S(1)}, bf16[2,2,2,3,128,128]{5,4,3,2,1,0:T(8,128)(2,1)}, u32[]{:S(2)}) copy-start(bf16[2,2,2,3,128,128]{5,4,3,2,1,0:T(8,128)(2,1)} %copy-done.4) | copy-start | bytes 2359300
  23.8 12.5 %collective-permute-start = (bf16[2,2,2,3,128,128]{5,4,3,2,1,0:T(8,128)(2,1)S(1)}, bf16[2,2,2,3,128,128]{5,4,3,2,1,0:T(8,128)(2,1)S(1)}, u32[]{:S(2)}, u32[]{:S(2)}) collective-permute-start(bf16[2,2,2,3,128,128]{5,4,3,2,1,0:T(8,128)(2,1)S(1)} %get-tuple-element.16), channel_id=1, source_target_pairs={{0,384},{384,0},{1,385},{385,1},{2,386},{386,2},{3,387},{387,3},{4... | collective-permute-start | bytes 2359304 | tf_op jit(solution)/shard_map/ppermute | solution.py:346
  34.4 4.2 %collective-permute-start.1 = (bf16[2,2,2,3,128,128]{5,4,3,2,1,0:T(8,128)(2,1)S(1)}, bf16[2,2,2,3,128,128]{5,4,3,2,1,0:T(8,128)(2,1)S(1)}, u32[]{:S(2)}, u32[]{:S(2)}) collective-permute-start(bf16[2,2,2,3,128,128]{5,4,3,2,1,0:T(8,128)(2,1)S(1)} %get-tuple-element.17), channel_id=1, source_target_pairs={{0,384},{384,0},{1,385},{385,1},{2,386},{386,2},{3,387},{387,3},{4... | collective-permute-start | bytes 2359304 | tf_op jit(solution)/shard_map/ppermute | solution.py:347
  36.3 0.9 %copy-start.6 = (bf16[2,2,2,3,128,128]{5,4,3,2,1,0:T(8,128)(2,1)}, bf16[2,2,2,3,128,128]{5,4,3,2,1,0:T(8,128)(2,1)S(1)}, u32[]{:S(2)}) copy-start(bf16[2,2,2,3,128,128]{5,4,3,2,1,0:T(8,128)(2,1)S(1)} %collective-permute-done.refs_1_) | copy-start | bytes 2359300
  41.4 29.8 %copy-start.3 = (bf16[2,2,2,3,128,128]{5,4,3,2,1,0:T(8,128)(2,1)S(1)}, bf16[2,2,2,3,128,128]{5,4,3,2,1,0:T(8,128)(2,1)}, u32[]{:S(2)}) copy-start(bf16[2,2,2,3,128,128]{5,4,3,2,1,0:T(8,128)(2,1)} %copy-done.2) | copy-start | bytes 2359300
  41.4 22.1 %all-to-all-start.1 = ((bf16[4,6,128,128]{3,2,1,0:T(8,128)(2,1)}), bf16[4,6,128,128]{3,2,1,0:T(8,128)(2,1)S(1)}, u32[]{:S(2)}, u32[]{:S(2)}) async-start(bf16[4,6,128,128]{3,2,1,0:T(8,128)(2,1)} %bitcast.7), calls=%async_computation.1 | async-start | bytes 1572864 | tf_op jit(solution)/shard_map/all_to_all | solution.py:352
  54.9 1.1 %copy-start.7 = (bf16[2,2,2,3,128,128]{5,4,3,2,1,0:T(8,128)(2,1)S(1)}, bf16[2,2,2,3,128,128]{5,4,3,2,1,0:T(8,128)(2,1)}, u32[]{:S(2)}) copy-start(bf16[2,2,2,3,128,128]{5,4,3,2,1,0:T(8,128)(2,1)} %copy-done.6) | copy-start | bytes 2359300
  57.1 14.1 %collective-permute-start.2 = (bf16[2,2,2,3,128,128]{5,4,3,2,1,0:T(8,128)(2,1)}, bf16[2,2,2,3,128,128]{5,4,3,2,1,0:T(8,128)(2,1)S(1)}, u32[]{:S(2)}, u32[]{:S(2)}) collective-permute-start(bf16[2,2,2,3,128,128]{5,4,3,2,1,0:T(8,128)(2,1)} %shard_map.108), channel_id=1, source_target_pairs={{0,96},{96,0},{192,288},{288,192},{384,672},{480,576},{576,480},{6... | collective-permute-start | bytes 2359304 | tf_op jit(solution)/shard_map/ppermute | solution.py:348
  64.3 20.5 %all-to-all-start.2 = ((bf16[6,128,128]{2,1,0:T(8,128)(2,1)}), bf16[6,128,128]{2,1,0:T(8,128)(2,1)S(1)}, u32[]{:S(2)}, u32[]{:S(2)}) async-start(bf16[6,128,128]{2,1,0:T(8,128)(2,1)} %shard_map.106), calls=%async_computation.2 | async-start | bytes 393216 | tf_op jit(solution)/shard_map/all_to_all | solution.py:364
  71.3 9.7 %collective-permute-start.3 = (bf16[1,2,2,3,128,128]{5,4,3,2,1,0:T(8,128)(2,1)S(1)}, bf16[1,2,2,3,128,128]{5,4,3,2,1,0:T(8,128)(2,1)S(1)}, u32[]{:S(2)}, u32[]{:S(2)}) collective-permute-start(bf16[1,2,2,3,128,128]{5,4,3,2,1,0:T(8,128)(2,1)S(1)} %shard_map.109), channel_id=1, source_target_pairs={{0,288},{96,192},{192,96},{288,0},{384,480},{480,384},{576,672},{6... | collective-permute-start | bytes 1179656 | tf_op jit(solution)/shard_map/ppermute | solution.py:359

commit v3 on v2

--- a/solution.py
+++ b/solution.py
@@ -96,45 +96,56 @@
 
 def forward_kernel(
     core, place_hbm, rows_hbm, cols_hbm, count_hbm, inputs_hbm, out_grad_hbm, ups_hbm, downs_hbm,
-    placed_hbm, hidden_t, pre_grad_t,
-    placed, inputs, out_grad, ups, downs, place, rows, cols, count, small_sems, sems, out_sem,
+    placed_hbm, hidden_t_hbm, pre_grad_t_hbm,
+    placed, hidden_t, pre_grad_t, inputs, out_grad, ups, downs, place, rows, cols, count, small_sems, sems, out_sems,
 ):
     slots, fan = rows.shape
     tok = inputs.shape[0]
-    small = [
-        pltpu.make_async_copy(source, target, small_sems.at[i])
-        for i, (source, target) in enumerate(
-            ((rows_hbm, rows), (cols_hbm, cols), (place_hbm, place), (count_hbm, count))
-        )
-    ]
-    large = [
-        pltpu.make_async_copy(source, target, sems.at[i])
-        for i, (source, target) in enumerate(
-            (
-                (ups_hbm.at[0], ups.at[0]),
-                (inputs_hbm, inputs),
-                (downs_hbm.at[0], downs.at[0]),
-                (out_grad_hbm, out_grad),
-                (ups_hbm.at[1], ups.at[1]),
-                (downs_hbm.at[1], downs.at[1]),
-            )
-        )
-    ]
+    half = BLK // 2
+
+    def copies_of(pairs, semaphores):
+        return [pltpu.make_async_copy(a, b, semaphores.at[i]) for i, (a, b) in enumerate(pairs)]
+
+    small = copies_of(((rows_hbm, rows), (cols_hbm, cols), (place_hbm, place), (count_hbm, count)), small_sems)
+    large = copies_of(
+        (
+            (ups_hbm.at[0], ups.at[0]),
+            (inputs_hbm, inputs),
+            (ups_hbm.at[1], ups.at[1]),
+            (downs_hbm.at[0], downs.at[0]),
+            (out_grad_hbm, out_grad),
+            (downs_hbm.at[1], downs.at[1]),
+        ),
+        sems,
+    )
+    written = copies_of(
+        (
+            (placed.at[:, pl.ds(0, half)], placed_hbm.at[:, pl.ds(0, half)]),
+            (placed.at[:, pl.ds(half, half)], placed_hbm.at[:, pl.ds(half, half)]),
+            (hidden_t, hidden_t_hbm),
+            (pre_grad_t, pre_grad_t_hbm),
+        ),
+        out_sems,
+    )
     for copy in small + large:
         copy.start()
     placed[...] = jnp.zeros_like(placed)
     for copy in small:
         copy.wait()
+    slopes = []
     for s in range(slots):
         live = (s < count[0]).astype(jnp.float32)
-        for copy in large[:2] if s == 0 else large[4:5]:
+        for copy in large[:2] if s == 0 else large[2:3]:
             copy.wait()
         pre_act = jnp.zeros((tok, BLK), jnp.float32)
         for k in range(0, fan, 2):
-            pre_act += dot_nn(
-                two_blocks(inputs, rows[s, k], rows[s, k + 1]), ups[s, k * BLK : (k + 2) * BLK, :]
-            )
-        for copy in large[2:4] if s == 0 else large[5:]:
+            pre_act += dot_nn(two_blocks(inputs, rows[s, k], rows[s, k + 1]), ups[s, k * BLK : (k + 2) * BLK, :])
+        value, slope = gelu_pair(pre_act)
+        hidden_t[s] = jnp.transpose(value * live).astype(jnp.bfloat16)
+        slopes.append(slope * live)
+    written[2].start()
+    for s in range(slots):
+        for copy in large[3:5] if s == 0 else large[5:]:
             copy.wait()
         hid_grad = jnp.zeros((tok, BLK), jnp.float32)
         for k in range(0, fan, 2):
@@ -142,21 +153,24 @@
                 two_blocks(out_grad, cols[s, k], cols[s, k + 1]),
                 jnp.concatenate([downs[s, k * BLK : (k + 1) * BLK, :], downs[s, (k + 1) * BLK : (k + 2) * BLK, :]], axis=1),
             )
-        value, slope = gelu_pair(pre_act)
-        hidden_t[s] = jnp.transpose(value * live).astype(jnp.bfloat16)
-        turned = jnp.transpose(hid_grad * slope * live).astype(jnp.bfloat16)
-        pre_grad_t[s] = turned
-        for k in range(0, fan, 2):
-            both = dot_nn(ups[s, k * BLK : (k + 2) * BLK, :], turned)
-            for i in range(2):
-                at = place[core[0], rows[s, k + i]]
-                product = both[i * BLK : (i + 1) * BLK, :]
-                if s > 0:
-                    product += placed[at].astype(jnp.float32)
-                placed[at] = product.astype(jnp.bfloat16)
-    write = pltpu.make_async_copy(placed, placed_hbm, out_sem)
-    write.start()
-    write.wait()
+        pre_grad_t[s] = jnp.transpose(hid_grad * slopes[s]).astype(jnp.bfloat16)
+    written[3].start()
+    for h in range(2):
+        part = slice(h * half, (h + 1) * half)
+        for s in range(slots):
+            turned = pre_grad_t[s]
+            for k in range(0, fan, 2):
+                edges = [(k + i) * BLK + h * half for i in range(2)]
+                both = dot_nn(jnp.concatenate([ups[s, e : e + half, :] for e in edges], axis=0), turned)
+                for i in range(2):
+                    at = place[core[0], rows[s, k + i]]
+                    product = both[i * half : (i + 1) * half, :]
+                    if s > 0:
+                        product += placed[at, part].astype(jnp.float32)
+                    placed[at, part] = product.astype(jnp.bfloat16)
+        written[h].start()
+    for copy in written:
+        copy.wait()
 
 
 def weight_kernel(
@@ -214,31 +228,43 @@
     return small_call(sum_first_kernel, jax.ShapeDtypeStruct(terms.shape[1:], terms.dtype), terms)
 
 
-def sum_large_kernel(terms_hbm, total, terms, sems):
-    steps = sems.shape[0]
-    rows = total.shape[0] // steps
-    pieces = [pl.ds(i * rows, rows) for i in range(steps)]
+def sum_large_kernel(terms_hbm, total_hbm, terms, total, sems, out_sems):
+    edges = [0, 6, 12, 17, 21, 24]
+    pieces = [pl.ds(a, b - a) for a, b in zip(edges, edges[1:])]
     copies = [
         pltpu.make_async_copy(terms_hbm.at[:, piece], terms.at[:, piece], sems.at[i])
         for i, piece in enumerate(pieces)
     ]
+    written = [
+        pltpu.make_async_copy(total.at[piece], total_hbm.at[piece], out_sems.at[i])
+        for i, piece in enumerate(pieces)
+    ]
     for copy in copies:
         copy.start()
-    for copy, piece in zip(copies, pieces):
+    for copy, write, piece in zip(copies, written, pieces):
         copy.wait()
         value = terms[0, piece].astype(jnp.float32)
         for i in range(1, terms.shape[0]):
             value += terms[i, piece].astype(jnp.float32)
         total[piece] = value.astype(jnp.bfloat16)
+        write.start()
+    for write in written:
+        write.wait()
 
 
 def sum_large(terms):
+    hbm = pl.BlockSpec(memory_space=pltpu.HBM)
     return pl.pallas_call(
         sum_large_kernel,
         out_shape=jax.ShapeDtypeStruct(terms.shape[1:], terms.dtype),
-        in_specs=[pl.BlockSpec(memory_space=pltpu.HBM)],
-        out_specs=pl.BlockSpec(memory_space=pltpu.VMEM),
-        scratch_shapes=[pltpu.VMEM(terms.shape, terms.dtype), pltpu.SemaphoreType.DMA((6,))],
+        in_specs=[hbm],
+        out_specs=hbm,
+        scratch_shapes=[
+            pltpu.VMEM(terms.shape, terms.dtype),
+            pltpu.VMEM(terms.shape[1:], terms.dtype),
+            pltpu.SemaphoreType.DMA((5,)),
+            pltpu.SemaphoreType.DMA((5,)),
+        ],
         compiler_params=pltpu.CompilerParams(vmem_limit_bytes=VMEM_LIMIT),
     )(terms)
 
@@ -297,9 +323,11 @@
             jax.ShapeDtypeStruct((slots, BLK, tok), bf16),
         ),
         in_specs=[smem] + [hbm] * 8,
-        out_specs=(hbm, vmem, vmem),
+        out_specs=(hbm,) * 3,
         scratch_shapes=[
             pltpu.VMEM((N_Y * N_Z, BLK, tok), bf16),
+            pltpu.VMEM((slots, BLK, tok), bf16),
+            pltpu.VMEM((slots, BLK, tok), bf16),
             pltpu.VMEM((tok, features), bf16),
             pltpu.VMEM((tok, features), bf16),
             pltpu.VMEM(wide, bf16),
@@ -310,7 +338,7 @@
             pltpu.SMEM((1,), jnp.int32),
             pltpu.SemaphoreType.DMA((4,)),
             pltpu.SemaphoreType.DMA((6,)),
-            pltpu.SemaphoreType.DMA(()),
+            pltpu.SemaphoreType.DMA((4,)),
         ],
         compiler_params=pltpu.CompilerParams(vmem_limit_bytes=VMEM_LIMIT),
     )(
@@ -345,10 +373,9 @@
     other_core = [(0, 1), (1, 0)]
     far_arrived = lax.ppermute(theirs_far, "dp", other_core)
     near_arrived = lax.ppermute(theirs_near, "dp", other_core)
-    first_got = lax.ppermute(
-        add_last(2, mine_far, far_arrived), TOKENS_AX, core_seq_pairs(lambda c, q: 3 - q if c else q ^ 1)
-    )
-    near, _, _ = lax.optimization_barrier((near, far_arrived, near_arrived))
+    first_sent = add_last(2, mine_far, far_arrived)
+    first_got = lax.ppermute(first_sent, TOKENS_AX, core_seq_pairs(lambda c, q: 3 - q if c else q ^ 1))
+    near, _, _ = lax.optimization_barrier((near, first_sent, near_arrived))
     mid = lax.all_to_all(
         sum_large(near).reshape(4, 6, BLK, tok),
         everyone,

time: 86.1 us -> 84.2 us (0.978)
  Pallas kernels: 18.8 us -> 16.2 us
  local copies, waits for them, and re-layouts: 5.77 us -> 3.71 us
  waiting for transfers between devices: 15.5 us -> 17.5 us
    all_to_all x1, waiting for transfers between devices: 3.33 us -> 5.54 us  [local(): lax.all_to_all(sum_large(near).reshape(4, 6, BLK, tok), everyone, 0, 0, a...]
    unnamed x24 -> x18, local copies, waits for them, and re-layouts: 5.77 us -> 3.71 us
    pallas_call x1, Pallas kernels: 8.46 us -> 7.04 us  [local(): pl.pallas_call(forward_kernel, out_shape=(jax.ShapeDtypeStruct((N_Y * N_Z...]
    pallas_call x5, Pallas kernels: 3.64 us -> 2.72 us  [small_call(): pl.pallas_call(kernel, out_shape=out_shape, in_specs=[vmem] * len(operand...]
    all_to_all x1, starting transfers between devices: 13.5 us -> 14.4 us  [local(): lax.all_to_all(sum_large(near).reshape(4, 6, BLK, tok), everyone, 0, 0, a...]
  transfers between devices with their start and end apart: 7 -> 7, of which waited for: 5 -> 4; matrix products, arithmetic and copies ran while one was open for 0% -> 0% of each run, Pallas kernels for 8% -> 7%
where the time goes in v3:
time: 84.2 us; the launch traced here: 83.7 us
  starting transfers between devices  44.8 us (53%)
  waiting for transfers between devices  17.5 us (21%)
  Pallas kernels  16.2 us (19%)
  local copies, waits for them, and re-layouts  3.71 us (4%)
  between operations  1.45 us (2%)
    all_to_all x1, starting transfers between devices, local(): lax.all_to_all(sum_large(near).reshape(4, 6, BLK, tok), everyone, 0, 0, a...  14.4 us
    ppermute x1, starting transfers between devices, local(): far_arrived = lax.ppermute(theirs_far, 'dp', other_core)  10.4 us
    ppermute x1, waiting for transfers between devices, local(): lax.ppermute(add_last(1, mine_near, near_arrived, first_got), TOKENS_AX,...  7.22 us
    pallas_call x1, Pallas kernels, local(): pl.pallas_call(forward_kernel, out_shape=(jax.ShapeDtypeStruct((N_Y * N_Z...  7.04 us
    all_to_all x1, starting transfers between devices, local(): lax.all_to_all(placed.reshape(4, 24, BLK, tok), everyone, 0, 0, axis_inde...  6.45 us
    all_to_all x1, starting transfers between devices, local(): lax.all_to_all(sum_first(mid), everyone, 0, 0, axis_index_groups=owner_gr...  6.12 us
    all_to_all x1, waiting for transfers between devices, local(): lax.all_to_all(sum_large(near).reshape(4, 6, BLK, tok), everyone, 0, 0, a...  5.54 us
    pallas_call x1, Pallas kernels, local(): pl.pallas_call(weight_kernel, out_shape=(part_shape,) * 4, in_specs=[smem...  3.84 us
  transfers between devices with their start and end apart: 7, of which 4 were waited for; matrix products, arithmetic and copies ran while one was open for 0% of the time, Pallas kernels for 7%

profile of v3, /device:TPU:20, one launch (start us, length us, event | category | flops | bytes accessed | tf_op | source)
XLA Modules:
  0.0 83.7 jit_solution(11769949299804550578)
XLA Ops:
  1.3 7.0 %shard_map.103 = (bf16[96,128,128]{2,1,0:T(8,128)(2,1)}, bf16[2,128,128]{2,1,0:T(8,128)(2,1)}, bf16[2,128,128]{2,1,0:T(8,128)(2,1)}) custom-call(s32[1]{0:T(128)} %bitcast.core, s32[2,96]{1,0:T(2,128)} %constant.18.place_hbm, s32[2,24]{1,0:T(2,128)} %rows.1, s32[2,24]{1,0:T(2,128)} %cols.1, s32[1]{0:T(128)S(6)} %copy.11.count_hbm, ...), custom_call_target="tpu_custom_call" | custom-call | tf_op jit(solution)/shard_map/pallas_call | solution.py:318
  8.3 0.0 copy-start
  8.3 0.0 copy-start.5
  8.4 0.0 copy-start.6
  8.4 0.0 copy-start.7
  8.4 0.0 copy-start.8
  8.4 6.4 %all-to-all-start = ((bf16[4,24,128,128]{3,2,1,0:T(8,128)(2,1)}), bf16[4,24,128,128]{3,2,1,0:T(8,128)(2,1)}, u32[]{:S(2)}, u32[]{:S(2)}) async-start(bf16[4,24,128,128]{3,2,1,0:T(8,128)(2,1)} %bitcast.6), calls=%async_computation | async-start | bytes 6291456 | tf_op jit(solution)/shard_map/all_to_all | solution.py:356
  14.8 0.0 copy-done
  14.9 0.0 copy-start.1
  14.9 1.9 %copy-done.1 = bf16[128,12288]{1,0:T(8,128)(2,1)S(1)} copy-done((bf16[128,12288]{1,0:T(8,128)(2,1)S(1)}, bf16[128,12288]{1,0:T(8,128)(2,1)}, u32[]{:S(2)}) %copy-start.1) | copy-done | bytes 3145752
  16.8 3.8 %shard_map.104 = (bf16[2,2,2,3,128,128]{5,4,3,2,1,0:T(8,128)(2,1)S(1)}, bf16[2,2,2,3,128,128]{5,4,3,2,1,0:T(8,128)(2,1)S(1)}, bf16[2,2,2,3,128,128]{5,4,3,2,1,0:...) custom-call(s32[1]{0:T(128)} %bitcast.core, s32[1]{0:T(128)} %bitcast.4.seq, s32[2,24]{1,0:T(2,128)S(1)} %copy-done.7, ...), custom_call_target="tpu_custom_call" | custom-call | flops 400000000 | bytes 10000000 | tf_op jit(solution)/shard_map/pallas_call | solution.py:361
  20.6 0.9 %copy-done.2 = bf16[2,2,2,3,128,128]{5,4,3,2,1,0:T(8,128)(2,1)} copy-done((bf16[2,2,2,3,128,128]{5,4,3,2,1,0:T(8,128)(2,1)}, bf16[2,2,2,3,128,128]{5,4,3,2,1,0:T(8,128)(2,1)S(1)}, u32[]{:S(2)}) %copy-start.2) | copy-done | bytes 786456
  21.5 10.4 %collective-permute-start = (bf16[2,2,2,3,128,128]{5,4,3,2,1,0:T(8,128)(2,1)S(1)}, bf16[2,2,2,3,128,128]{5,4,3,2,1,0:T(8,128)(2,1)S(1)}, u32[]{:S(2)}, u32[]{:S(2)}) collective-permute-start(bf16[2,2,2,3,128,128]{5,4,3,2,1,0:T(8,128)(2,1)S(1)} %get-tuple-element.17), channel_id=1, source_target_pairs={{0,384},{384,0},{1,385},{385,1},{2,386},{386,2},{3,387},{387,3},{4... | collective-permute-start | bytes 2359304 | tf_op jit(solution)/shard_map/ppermute | solution.py:374
  31.9 1.9 %collective-permute-start.1 = (bf16[2,2,2,3,128,128]{5,4,3,2,1,0:T(8,128)(2,1)S(1)}, bf16[2,2,2,3,128,128]{5,4,3,2,1,0:T(8,128)(2,1)S(1)}, u32[]{:S(2)}, u32[]{:S(2)}) collective-permute-start(bf16[2,2,2,3,128,128]{5,4,3,2,1,0:T(8,128)(2,1)S(1)} %get-tuple-element.18), channel_id=1, source_target_pairs={{0,384},{384,0},{1,385},{385,1},{2,386},{386,2},{3,387},{387,3},{4... | collective-permute-start | bytes 2359304 | tf_op jit(solution)/shard_map/ppermute | solution.py:375
  33.9 0.0 collective-permute-done.refs_1_
  33.9 0.2 shard_map.105
  34.1 0.9 %copy-done.4 = bf16[2,2,2,3,128,128]{5,4,3,2,1,0:T(8,128)(2,1)} copy-done((bf16[2,2,2,3,128,128]{5,4,3,2,1,0:T(8,128)(2,1)}, bf16[2,2,2,3,128,128]{5,4,3,2,1,0:T(8,128)(2,1)S(1)}, u32[]{:S(2)}) %copy-start.4) | copy-done | bytes 786456
  35.0 1.2 %collective-permute-done.1.refs_1_ = bf16[2,2,2,3,128,128]{5,4,3,2,1,0:T(8,128)(2,1)S(1)} collective-permute-done((bf16[2,2,2,3,128,128]{5,4,3,2,1,0:T(8,128)(2,1)S(1)}, bf16[2,2,2,3,128,128]{5,4,3,2,1,0:T(8,128)(2,1)S(1)}, u32[]{:S(2)}, u32[]{:S(2)}) %collective-permute-start.1) | collective-permute-done | bytes 786464 | tf_op jit(solution)/shard_map/ppermute | solution.py:375
  36.1 0.0 all-to-all-done.terms_hbm
  36.1 2.6 %shard_map.106 = bf16[24,128,128]{2,1,0:T(8,128)(2,1)} custom-call(bf16[4,24,128,128]{3,2,1,0:T(8,128)(2,1)} %all-to-all-done.terms_hbm), custom_call_target="tpu_custom_call" | custom-call | tf_op jit(solution)/shard_map/pallas_call | solution.py:257
  38.7 14.4 %all-to-all-start.1 = ((bf16[4,6,128,128]{3,2,1,0:T(8,128)(2,1)}), bf16[4,6,128,128]{3,2,1,0:T(8,128)(2,1)S(1)}, u32[]{:S(2)}, u32[]{:S(2)}) async-start(bf16[4,6,128,128]{3,2,1,0:T(8,128)(2,1)} %bitcast.7), calls=%async_computation.1 | async-start | bytes 1572864 | tf_op jit(solution)/shard_map/all_to_all | solution.py:379
  53.1 3.1 %collective-permute-start.2 = (bf16[2,2,2,3,128,128]{5,4,3,2,1,0:T(8,128)(2,1)}, bf16[2,2,2,3,128,128]{5,4,3,2,1,0:T(8,128)(2,1)S(1)}, u32[]{:S(2)}, u32[]{:S(2)}) collective-permute-start(bf16[2,2,2,3,128,128]{5,4,3,2,1,0:T(8,128)(2,1)} %copy-done.4), channel_id=1, source_target_pairs={{0,96},{96,0},{192,288},{288,192},{384,672},{480,576},{576,480},{6... | collective-permute-start | bytes 2359304 | tf_op jit(solution)/shard_map/ppermute | solution.py:377
  56.2 5.5 %all-to-all-done.1.terms = bf16[4,6,128,128]{3,2,1,0:T(8,128)(2,1)S(1)} async-done(((bf16[4,6,128,128]{3,2,1,0:T(8,128)(2,1)}), bf16[4,6,128,128]{3,2,1,0:T(8,128)(2,1)S(1)}, u32[]{:S(2)}, u32[]{:S(2)}) %all-to-all-start.1) | async-done | bytes 786464 | tf_op jit(solution)/shard_map/all_to_all | solution.py:379
  61.7 0.8 shard_map.107
  62.5 6.1 %all-to-all-start.2 = ((bf16[6,128,128]{2,1,0:T(8,128)(2,1)}), bf16[6,128,128]{2,1,0:T(8,128)(2,1)S(1)}, u32[]{:S(2)}, u32[]{:S(2)}) async-start(bf16[6,128,128]{2,1,0:T(8,128)(2,1)} %shard_map.107), calls=%async_computation.2 | async-start | bytes 393216 | tf_op jit(solution)/shard_map/all_to_all | solution.py:391
  68.6 0.0 collective-permute-done.2.refs_2_
  68.6 0.1 shard_map.109
  68.8 2.4 %collective-permute-start.3 = (bf16[1,2,2,3,128,128]{5,4,3,2,1,0:T(8,128)(2,1)S(1)}, bf16[1,2,2,3,128,128]{5,4,3,2,1,0:T(8,128)(2,1)S(1)}, u32[]{:S(2)}, u32[]{:S(2)}) collective-permute-start(bf16[1,2,2,3,128,128]{5,4,3,2,1,0:T(8,128)(2,1)S(1)} %shard_map.109), channel_id=1, source_target_pairs={{0,288},{96,192},{192,96},{288,0},{384,480},{480,384},{576,672},{6... | collective-permute-start | bytes 1179656 | tf_op jit(solution)/shard_map/ppermute | solution.py:386
  71.2 7.2 %collective-permute-done.3.refs_3_ = bf16[1,2,2,3,128,128]{5,4,3,2,1,0:T(8,128)(2,1)S(1)} collective-permute-done((bf16[1,2,2,3,128,128]{5,4,3,2,1,0:T(8,128)(2,1)S(1)}, bf16[1,2,2,3,128,128]{5,4,3,2,1,0:T(8,128)(2,1)S(1)}, u32[]{:S(2)}, u32[]{:S(2)}) %collective-permute-start.3) | collective-permute-done | bytes 393248 | tf_op jit(solution)/shard_map/ppermute | solution.py:386
  78.4 0.9 %shard_map.110 = (bf16[2,3,128,128]{3,2,1,0:T(8,128)(2,1)}, bf16[2,3,128,128]{3,2,1,0:T(8,128)(2,1)}) custom-call(bf16[2,2,2,3,128,128]{5,4,3,2,1,0:T(8,128)(2,1)S(1)} %copy-done.3, bf16[2,2,2,3,128,128]{5,4,3,2,1,0:T(8,128)(2,1)S(1)} %collective-permute-done.1.refs_1_, bf16[2,2,2,3,128,128]{5,4,3,2,1,0:T(8,128)(2,1)S(1)} %collective-permute-done.2.refs_2_, ...), custom_call_target="tpu_custom_call" | custom-call | tf_op jit(solution)/shard_map/pallas_call | solution.py:211
  79.4 3.6 %all-to-all-done.2.terms = bf16[6,128,128]{2,1,0:T(8,128)(2,1)S(1)} async-done(((bf16[6,128,128]{2,1,0:T(8,128)(2,1)}), bf16[6,128,128]{2,1,0:T(8,128)(2,1)S(1)}, u32[]{:S(2)}, u32[]{:S(2)}) %all-to-all-start.2) | async-done | bytes 196640 | tf_op jit(solution)/shard_map/all_to_all | solution.py:391
  83.0 0.7 shard_map.108
  (8 shorter events, 0.0 us)
Async XLA Ops:
  8.3 6.5 %copy-start = (bf16[128,12288]{1,0:T(8,128)(2,1)S(1)}, bf16[128,12288]{1,0:T(8,128)(2,1)}, u32[]{:S(2)}) copy-start(bf16[128,12288]{1,0:T(8,128)(2,1)} %inputs.1) | copy-start | bytes 9437188
  8.3 6.5 %copy-start.5 = (bf16[2,128,128]{2,1,0:T(8,128)(2,1)S(1)}, bf16[2,128,128]{2,1,0:T(8,128)(2,1)}, u32[]{:S(2)}) copy-start(bf16[2,128,128]{2,1,0:T(8,128)(2,1)} %get-tuple-element.14.hidden_t) | copy-start | bytes 196612
  8.4 6.5 %copy-start.6 = (bf16[2,128,128]{2,1,0:T(8,128)(2,1)S(1)}, bf16[2,128,128]{2,1,0:T(8,128)(2,1)}, u32[]{:S(2)}) copy-start(bf16[2,128,128]{2,1,0:T(8,128)(2,1)} %get-tuple-element.15.pre_grad_t) | copy-start | bytes 196612
  8.4 6.5 %copy-start.7 = (s32[2,24]{1,0:T(2,128)S(1)}, s32[2,24]{1,0:T(2,128)}, u32[]{:S(2)}) copy-start(s32[2,24]{1,0:T(2,128)} %rows.1) | copy-start | bytes 580
  8.4 6.5 %copy-start.8 = (s32[2,24]{1,0:T(2,128)S(1)}, s32[2,24]{1,0:T(2,128)}, u32[]{:S(2)}) copy-start(s32[2,24]{1,0:T(2,128)} %cols.1) | copy-start | bytes 580
  8.4 27.7 %all-to-all-start = ((bf16[4,24,128,128]{3,2,1,0:T(8,128)(2,1)}), bf16[4,24,128,128]{3,2,1,0:T(8,128)(2,1)}, u32[]{:S(2)}, u32[]{:S(2)}) async-start(bf16[4,24,128,128]{3,2,1,0:T(8,128)(2,1)} %bitcast.6), calls=%async_computation | async-start | bytes 6291456 | tf_op jit(solution)/shard_map/all_to_all | solution.py:356
  14.9 1.9 %copy-start.1 = (bf16[128,12288]{1,0:T(8,128)(2,1)S(1)}, bf16[128,12288]{1,0:T(8,128)(2,1)}, u32[]{:S(2)}) copy-start(bf16[128,12288]{1,0:T(8,128)(2,1)} %out_grad.1) | copy-start | bytes 9437188
  20.6 0.9 %copy-start.2 = (bf16[2,2,2,3,128,128]{5,4,3,2,1,0:T(8,128)(2,1)}, bf16[2,2,2,3,128,128]{5,4,3,2,1,0:T(8,128)(2,1)S(1)}, u32[]{:S(2)}) copy-start(bf16[2,2,2,3,128,128]{5,4,3,2,1,0:T(8,128)(2,1)S(1)} %get-tuple-element.20.refs_0_) | copy-start | bytes 2359300
  21.5 12.3 %collective-permute-start = (bf16[2,2,2,3,128,128]{5,4,3,2,1,0:T(8,128)(2,1)S(1)}, bf16[2,2,2,3,128,128]{5,4,3,2,1,0:T(8,128)(2,1)S(1)}, u32[]{:S(2)}, u32[]{:S(2)}) collective-permute-start(bf16[2,2,2,3,128,128]{5,4,3,2,1,0:T(8,128)(2,1)S(1)} %get-tuple-element.17), channel_id=1, source_target_pairs={{0,384},{384,0},{1,385},{385,1},{2,386},{386,2},{3,387},{387,3},{4... | collective-permute-start | bytes 2359304 | tf_op jit(solution)/shard_map/ppermute | solution.py:374
  31.9 4.2 %collective-permute-start.1 = (bf16[2,2,2,3,128,128]{5,4,3,2,1,0:T(8,128)(2,1)S(1)}, bf16[2,2,2,3,128,128]{5,4,3,2,1,0:T(8,128)(2,1)S(1)}, u32[]{:S(2)}, u32[]{:S(2)}) collective-permute-start(bf16[2,2,2,3,128,128]{5,4,3,2,1,0:T(8,128)(2,1)S(1)} %get-tuple-element.18), channel_id=1, source_target_pairs={{0,384},{384,0},{1,385},{385,1},{2,386},{386,2},{3,387},{387,3},{4... | collective-permute-start | bytes 2359304 | tf_op jit(solution)/shard_map/ppermute | solution.py:375
  34.1 0.9 %copy-start.4 = (bf16[2,2,2,3,128,128]{5,4,3,2,1,0:T(8,128)(2,1)}, bf16[2,2,2,3,128,128]{5,4,3,2,1,0:T(8,128)(2,1)S(1)}, u32[]{:S(2)}) copy-start(bf16[2,2,2,3,128,128]{5,4,3,2,1,0:T(8,128)(2,1)S(1)} %shard_map.105) | copy-start | bytes 2359300
  35.0 33.7 %copy-start.3 = (bf16[2,2,2,3,128,128]{5,4,3,2,1,0:T(8,128)(2,1)S(1)}, bf16[2,2,2,3,128,128]{5,4,3,2,1,0:T(8,128)(2,1)}, u32[]{:S(2)}) copy-start(bf16[2,2,2,3,128,128]{5,4,3,2,1,0:T(8,128)(2,1)} %copy-done.2) | copy-start | bytes 2359300
  38.7 23.0 %all-to-all-start.1 = ((bf16[4,6,128,128]{3,2,1,0:T(8,128)(2,1)}), bf16[4,6,128,128]{3,2,1,0:T(8,128)(2,1)S(1)}, u32[]{:S(2)}, u32[]{:S(2)}) async-start(bf16[4,6,128,128]{3,2,1,0:T(8,128)(2,1)} %bitcast.7), calls=%async_computation.1 | async-start | bytes 1572864 | tf_op jit(solution)/shard_map/all_to_all | solution.py:379
  53.1 15.5 %collective-permute-start.2 = (bf16[2,2,2,3,128,128]{5,4,3,2,1,0:T(8,128)(2,1)}, bf16[2,2,2,3,128,128]{5,4,3,2,1,0:T(8,128)(2,1)S(1)}, u32[]{:S(2)}, u32[]{:S(2)}) collective-permute-start(bf16[2,2,2,3,128,128]{5,4,3,2,1,0:T(8,128)(2,1)} %copy-done.4), channel_id=1, source_target_pairs={{0,96},{96,0},{192,288},{288,192},{384,672},{480,576},{576,480},{6... | collective-permute-start | bytes 2359304 | tf_op jit(solution)/shard_map/ppermute | solution.py:377
  62.5 20.5 %all-to-all-start.2 = ((bf16[6,128,128]{2,1,0:T(8,128)(2,1)}), bf16[6,128,128]{2,1,0:T(8,128)(2,1)S(1)}, u32[]{:S(2)}, u32[]{:S(2)}) async-start(bf16[6,128,128]{2,1,0:T(8,128)(2,1)} %shard_map.107), calls=%async_computation.2 | async-start | bytes 393216 | tf_op jit(solution)/shard_map/all_to_all | solution.py:391
  68.8 9.7 %collective-permute-start.3 = (bf16[1,2,2,3,128,128]{5,4,3,2,1,0:T(8,128)(2,1)S(1)}, bf16[1,2,2,3,128,128]{5,4,3,2,1,0:T(8,128)(2,1)S(1)}, u32[]{:S(2)}, u32[]{:S(2)}) collective-permute-start(bf16[1,2,2,3,128,128]{5,4,3,2,1,0:T(8,128)(2,1)S(1)} %shard_map.109), channel_id=1, source_target_pairs={{0,288},{96,192},{192,96},{288,0},{384,480},{480,384},{576,672},{6... | collective-permute-start | bytes 1179656 | tf_op jit(solution)/shard_map/ppermute | solution.py:386

commit v4 on v3

--- a/solution.py
+++ b/solution.py
@@ -101,7 +101,7 @@
 ):
     slots, fan = rows.shape
     tok = inputs.shape[0]
-    half = BLK // 2
+    quarter = BLK // 4
 
     def copies_of(pairs, semaphores):
         return [pltpu.make_async_copy(a, b, semaphores.at[i]) for i, (a, b) in enumerate(pairs)]
@@ -109,22 +109,18 @@
     small = copies_of(((rows_hbm, rows), (cols_hbm, cols), (place_hbm, place), (count_hbm, count)), small_sems)
     large = copies_of(
         (
+            (inputs_hbm, inputs),
             (ups_hbm.at[0], ups.at[0]),
-            (inputs_hbm, inputs),
             (ups_hbm.at[1], ups.at[1]),
+            (out_grad_hbm, out_grad),
             (downs_hbm.at[0], downs.at[0]),
-            (out_grad_hbm, out_grad),
             (downs_hbm.at[1], downs.at[1]),
         ),
         sems,
     )
     written = copies_of(
-        (
-            (placed.at[:, pl.ds(0, half)], placed_hbm.at[:, pl.ds(0, half)]),
-            (placed.at[:, pl.ds(half, half)], placed_hbm.at[:, pl.ds(half, half)]),
-            (hidden_t, hidden_t_hbm),
-            (pre_grad_t, pre_grad_t_hbm),
-        ),
+        [(placed.at[:, pl.ds(h * quarter, quarter)], placed_hbm.at[:, pl.ds(h * quarter, quarter)]) for h in range(4)]
+        + [(hidden_t, hidden_t_hbm), (pre_grad_t, pre_grad_t_hbm)],
         out_sems,
     )
     for copy in small + large:
@@ -143,7 +139,7 @@
         value, slope = gelu_pair(pre_act)
         hidden_t[s] = jnp.transpose(value * live).astype(jnp.bfloat16)
         slopes.append(slope * live)
-    written[2].start()
+    written[4].start()
     for s in range(slots):
         for copy in large[3:5] if s == 0 else large[5:]:
             copy.wait()
@@ -154,17 +150,17 @@
                 jnp.concatenate([downs[s, k * BLK : (k + 1) * BLK, :], downs[s, (k + 1) * BLK : (k + 2) * BLK, :]], axis=1),
             )
         pre_grad_t[s] = jnp.transpose(hid_grad * slopes[s]).astype(jnp.bfloat16)
-    written[3].start()
-    for h in range(2):
-        part = slice(h * half, (h + 1) * half)
+    written[5].start()
+    for h in range(4):
+        part = slice(h * quarter, (h + 1) * quarter)
         for s in range(slots):
             turned = pre_grad_t[s]
-            for k in range(0, fan, 2):
-                edges = [(k + i) * BLK + h * half for i in range(2)]
-                both = dot_nn(jnp.concatenate([ups[s, e : e + half, :] for e in edges], axis=0), turned)
-                for i in range(2):
+            for k in range(0, fan, 4):
+                edges = [(k + i) * BLK + h * quarter for i in range(4)]
+                both = dot_nn(jnp.concatenate([ups[s, e : e + quarter, :] for e in edges], axis=0), turned)
+                for i in range(4):
                     at = place[core[0], rows[s, k + i]]
-                    product = both[i * half : (i + 1) * half, :]
+                    product = both[i * quarter : (i + 1) * quarter, :]
                     if s > 0:
                         product += placed[at, part].astype(jnp.float32)
                     placed[at, part] = product.astype(jnp.bfloat16)
@@ -338,7 +334,7 @@
             pltpu.SMEM((1,), jnp.int32),
             pltpu.SemaphoreType.DMA((4,)),
             pltpu.SemaphoreType.DMA((6,)),
-            pltpu.SemaphoreType.DMA((4,)),
+            pltpu.SemaphoreType.DMA((6,)),
         ],
         compiler_params=pltpu.CompilerParams(vmem_limit_bytes=VMEM_LIMIT),
     )(

time: 84.2 us -> 84 us (level)
  the two profiles are of different devices: /device:TPU:20 before, /device:TPU:16 now
where the time goes in v4:
time: 84 us; the launch traced here: 83.5 us
  starting transfers between devices  47.3 us (56%)
  Pallas kernels  16 us (19%)
  waiting for transfers between devices  15 us (18%)
  local copies, waits for them, and re-layouts  3.71 us (4%)
  between operations  1.45 us (2%)
    all_to_all x1, starting transfers between devices, local(): lax.all_to_all(sum_large(near).reshape(4, 6, BLK, tok), everyone, 0, 0, a...  14.4 us
    ppermute x1, starting transfers between devices, local(): far_arrived = lax.ppermute(theirs_far, 'dp', other_core)  10.4 us
    pallas_call x1, Pallas kernels, local(): pl.pallas_call(forward_kernel, out_shape=(jax.ShapeDtypeStruct((N_Y * N_Z...  6.87 us
    all_to_all x1, starting transfers between devices, local(): lax.all_to_all(placed.reshape(4, 24, BLK, tok), everyone, 0, 0, axis_inde...  6.45 us
    ppermute x1, waiting for transfers between devices, local(): lax.ppermute(add_last(1, mine_near, near_arrived, first_got), TOKENS_AX,...  6.21 us
    all_to_all x1, starting transfers between devices, local(): lax.all_to_all(sum_first(mid), everyone, 0, 0, axis_index_groups=owner_gr...  6.13 us
    all_to_all x1, waiting for transfers between devices, local(): lax.all_to_all(sum_large(near).reshape(4, 6, BLK, tok), everyone, 0, 0, a...  5.24 us
    ppermute x1, starting transfers between devices, local(): lax.ppermute(add_last(1, mine_near, near_arrived, first_got), TOKENS_AX,...  4.67 us
  transfers between devices with their start and end apart: 7, of which 4 were waited for; matrix products, arithmetic and copies ran while one was open for 0% of the time, Pallas kernels for 7%

profile of v4, /device:TPU:16, one launch (start us, length us, event | category | flops | bytes accessed | tf_op | source)
XLA Modules:
  0.0 83.5 jit_solution(10032147395885388345)
XLA Ops:
  1.3 6.9 %shard_map.103 = (bf16[96,128,128]{2,1,0:T(8,128)(2,1)}, bf16[2,128,128]{2,1,0:T(8,128)(2,1)}, bf16[2,128,128]{2,1,0:T(8,128)(2,1)}) custom-call(s32[1]{0:T(128)} %bitcast.core, s32[2,96]{1,0:T(2,128)} %constant.18.place_hbm, s32[2,24]{1,0:T(2,128)} %rows.1, s32[2,24]{1,0:T(2,128)} %cols.1, s32[1]{0:T(128)S(6)} %copy.11.count_hbm, ...), custom_call_target="tpu_custom_call" | custom-call | tf_op jit(solution)/shard_map/pallas_call | solution.py:314
  8.2 0.0 copy-start
  8.2 0.0 copy-start.5
  8.2 0.0 copy-start.6
  8.2 0.0 copy-start.7
  8.2 0.0 copy-start.8
  8.2 6.5 %all-to-all-start = ((bf16[4,24,128,128]{3,2,1,0:T(8,128)(2,1)}), bf16[4,24,128,128]{3,2,1,0:T(8,128)(2,1)}, u32[]{:S(2)}, u32[]{:S(2)}) async-start(bf16[4,24,128,128]{3,2,1,0:T(8,128)(2,1)} %bitcast.6), calls=%async_computation | async-start | bytes 6291456 | tf_op jit(solution)/shard_map/all_to_all | solution.py:352
  14.7 0.0 copy-start.1
  14.7 1.9 %copy-done.1 = bf16[128,12288]{1,0:T(8,128)(2,1)S(1)} copy-done((bf16[128,12288]{1,0:T(8,128)(2,1)S(1)}, bf16[128,12288]{1,0:T(8,128)(2,1)}, u32[]{:S(2)}) %copy-start.1) | copy-done | bytes 3145752
  16.6 3.8 %shard_map.104 = (bf16[2,2,2,3,128,128]{5,4,3,2,1,0:T(8,128)(2,1)S(1)}, bf16[2,2,2,3,128,128]{5,4,3,2,1,0:T(8,128)(2,1)S(1)}, bf16[2,2,2,3,128,128]{5,4,3,2,1,0:...) custom-call(s32[1]{0:T(128)} %bitcast.core, s32[1]{0:T(128)} %bitcast.4.seq, s32[2,24]{1,0:T(2,128)S(1)} %copy-done.7, ...), custom_call_target="tpu_custom_call" | custom-call | flops 400000000 | bytes 10000000 | tf_op jit(solution)/shard_map/pallas_call | solution.py:357
  20.4 0.9 %copy-done.2 = bf16[2,2,2,3,128,128]{5,4,3,2,1,0:T(8,128)(2,1)} copy-done((bf16[2,2,2,3,128,128]{5,4,3,2,1,0:T(8,128)(2,1)}, bf16[2,2,2,3,128,128]{5,4,3,2,1,0:T(8,128)(2,1)S(1)}, u32[]{:S(2)}) %copy-start.2) | copy-done | bytes 786456
  21.4 10.4 %collective-permute-start = (bf16[2,2,2,3,128,128]{5,4,3,2,1,0:T(8,128)(2,1)S(1)}, bf16[2,2,2,3,128,128]{5,4,3,2,1,0:T(8,128)(2,1)S(1)}, u32[]{:S(2)}, u32[]{:S(2)}) collective-permute-start(bf16[2,2,2,3,128,128]{5,4,3,2,1,0:T(8,128)(2,1)S(1)} %get-tuple-element.17), channel_id=1, source_target_pairs={{0,384},{384,0},{1,385},{385,1},{2,386},{386,2},{3,387},{387,3},{4... | collective-permute-start | bytes 2359304 | tf_op jit(solution)/shard_map/ppermute | solution.py:370
  31.8 1.9 %collective-permute-start.1 = (bf16[2,2,2,3,128,128]{5,4,3,2,1,0:T(8,128)(2,1)S(1)}, bf16[2,2,2,3,128,128]{5,4,3,2,1,0:T(8,128)(2,1)S(1)}, u32[]{:S(2)}, u32[]{:S(2)}) collective-permute-start(bf16[2,2,2,3,128,128]{5,4,3,2,1,0:T(8,128)(2,1)S(1)} %get-tuple-element.18), channel_id=1, source_target_pairs={{0,384},{384,0},{1,385},{385,1},{2,386},{386,2},{3,387},{387,3},{4... | collective-permute-start | bytes 2359304 | tf_op jit(solution)/shard_map/ppermute | solution.py:371
  33.7 0.0 collective-permute-done.refs_1_
  33.7 0.2 shard_map.105
  33.9 0.0 copy-start.4
  33.9 0.9 %copy-done.4 = bf16[2,2,2,3,128,128]{5,4,3,2,1,0:T(8,128)(2,1)} copy-done((bf16[2,2,2,3,128,128]{5,4,3,2,1,0:T(8,128)(2,1)}, bf16[2,2,2,3,128,128]{5,4,3,2,1,0:T(8,128)(2,1)S(1)}, u32[]{:S(2)}) %copy-start.4) | copy-done | bytes 786456
  34.8 1.2 %collective-permute-done.1.refs_1_ = bf16[2,2,2,3,128,128]{5,4,3,2,1,0:T(8,128)(2,1)S(1)} collective-permute-done((bf16[2,2,2,3,128,128]{5,4,3,2,1,0:T(8,128)(2,1)S(1)}, bf16[2,2,2,3,128,128]{5,4,3,2,1,0:T(8,128)(2,1)S(1)}, u32[]{:S(2)}, u32[]{:S(2)}) %collective-permute-start.1) | collective-permute-done | bytes 786464 | tf_op jit(solution)/shard_map/ppermute | solution.py:371
  35.9 0.0 all-to-all-done.terms_hbm
  35.9 2.6 %shard_map.106 = bf16[24,128,128]{2,1,0:T(8,128)(2,1)} custom-call(bf16[4,24,128,128]{3,2,1,0:T(8,128)(2,1)} %all-to-all-done.terms_hbm), custom_call_target="tpu_custom_call" | custom-call | tf_op jit(solution)/shard_map/pallas_call | solution.py:253
  38.6 14.4 %all-to-all-start.1 = ((bf16[4,6,128,128]{3,2,1,0:T(8,128)(2,1)}), bf16[4,6,128,128]{3,2,1,0:T(8,128)(2,1)S(1)}, u32[]{:S(2)}, u32[]{:S(2)}) async-start(bf16[4,6,128,128]{3,2,1,0:T(8,128)(2,1)} %bitcast.7), calls=%async_computation.1 | async-start | bytes 1572864 | tf_op jit(solution)/shard_map/all_to_all | solution.py:375
  52.9 3.4 %collective-permute-start.2 = (bf16[2,2,2,3,128,128]{5,4,3,2,1,0:T(8,128)(2,1)}, bf16[2,2,2,3,128,128]{5,4,3,2,1,0:T(8,128)(2,1)S(1)}, u32[]{:S(2)}, u32[]{:S(2)}) collective-permute-start(bf16[2,2,2,3,128,128]{5,4,3,2,1,0:T(8,128)(2,1)} %copy-done.4), channel_id=1, source_target_pairs={{0,96},{96,0},{192,288},{288,192},{384,672},{480,576},{576,480},{6... | collective-permute-start | bytes 2359304 | tf_op jit(solution)/shard_map/ppermute | solution.py:373
  56.3 5.2 %all-to-all-done.1.terms = bf16[4,6,128,128]{3,2,1,0:T(8,128)(2,1)S(1)} async-done(((bf16[4,6,128,128]{3,2,1,0:T(8,128)(2,1)}), bf16[4,6,128,128]{3,2,1,0:T(8,128)(2,1)S(1)}, u32[]{:S(2)}, u32[]{:S(2)}) %all-to-all-start.1) | async-done | bytes 786464 | tf_op jit(solution)/shard_map/all_to_all | solution.py:375
  61.5 0.8 shard_map.107
  62.3 6.1 %all-to-all-start.2 = ((bf16[6,128,128]{2,1,0:T(8,128)(2,1)}), bf16[6,128,128]{2,1,0:T(8,128)(2,1)S(1)}, u32[]{:S(2)}, u32[]{:S(2)}) async-start(bf16[6,128,128]{2,1,0:T(8,128)(2,1)} %shard_map.107), calls=%async_computation.2 | async-start | bytes 393216 | tf_op jit(solution)/shard_map/all_to_all | solution.py:387
  68.4 0.0 collective-permute-done.2.refs_2_
  68.4 0.1 shard_map.109
  68.6 4.7 %collective-permute-start.3 = (bf16[1,2,2,3,128,128]{5,4,3,2,1,0:T(8,128)(2,1)S(1)}, bf16[1,2,2,3,128,128]{5,4,3,2,1,0:T(8,128)(2,1)S(1)}, u32[]{:S(2)}, u32[]{:S(2)}) collective-permute-start(bf16[1,2,2,3,128,128]{5,4,3,2,1,0:T(8,128)(2,1)S(1)} %shard_map.109), channel_id=1, source_target_pairs={{0,288},{96,192},{192,96},{288,0},{384,480},{480,384},{576,672},{6... | collective-permute-start | bytes 1179656 | tf_op jit(solution)/shard_map/ppermute | solution.py:382
  73.3 6.2 %collective-permute-done.3.refs_3_ = bf16[1,2,2,3,128,128]{5,4,3,2,1,0:T(8,128)(2,1)S(1)} collective-permute-done((bf16[1,2,2,3,128,128]{5,4,3,2,1,0:T(8,128)(2,1)S(1)}, bf16[1,2,2,3,128,128]{5,4,3,2,1,0:T(8,128)(2,1)S(1)}, u32[]{:S(2)}, u32[]{:S(2)}) %collective-permute-start.3) | collective-permute-done | bytes 393248 | tf_op jit(solution)/shard_map/ppermute | solution.py:382
  79.5 0.9 %shard_map.110 = (bf16[2,3,128,128]{3,2,1,0:T(8,128)(2,1)}, bf16[2,3,128,128]{3,2,1,0:T(8,128)(2,1)}) custom-call(bf16[2,2,2,3,128,128]{5,4,3,2,1,0:T(8,128)(2,1)S(1)} %copy-done.3, bf16[2,2,2,3,128,128]{5,4,3,2,1,0:T(8,128)(2,1)S(1)} %collective-permute-done.1.refs_1_, bf16[2,2,2,3,128,128]{5,4,3,2,1,0:T(8,128)(2,1)S(1)} %collective-permute-done.2.refs_2_, ...), custom_call_target="tpu_custom_call" | custom-call | tf_op jit(solution)/shard_map/pallas_call | solution.py:207
  80.4 2.4 %all-to-all-done.2.terms = bf16[6,128,128]{2,1,0:T(8,128)(2,1)S(1)} async-done(((bf16[6,128,128]{2,1,0:T(8,128)(2,1)}), bf16[6,128,128]{2,1,0:T(8,128)(2,1)S(1)}, u32[]{:S(2)}, u32[]{:S(2)}) %all-to-all-start.2) | async-done | bytes 196640 | tf_op jit(solution)/shard_map/all_to_all | solution.py:387
  82.8 0.7 shard_map.108
  (8 shorter events, 0.0 us)
Async XLA Ops:
  8.2 6.5 %copy-start = (bf16[128,12288]{1,0:T(8,128)(2,1)S(1)}, bf16[128,12288]{1,0:T(8,128)(2,1)}, u32[]{:S(2)}) copy-start(bf16[128,12288]{1,0:T(8,128)(2,1)} %inputs.1) | copy-start | bytes 9437188
  8.2 6.5 %copy-start.5 = (bf16[2,128,128]{2,1,0:T(8,128)(2,1)S(1)}, bf16[2,128,128]{2,1,0:T(8,128)(2,1)}, u32[]{:S(2)}) copy-start(bf16[2,128,128]{2,1,0:T(8,128)(2,1)} %get-tuple-element.14.hidden_t) | copy-start | bytes 196612
  8.2 6.5 %copy-start.6 = (bf16[2,128,128]{2,1,0:T(8,128)(2,1)S(1)}, bf16[2,128,128]{2,1,0:T(8,128)(2,1)}, u32[]{:S(2)}) copy-start(bf16[2,128,128]{2,1,0:T(8,128)(2,1)} %get-tuple-element.15.pre_grad_t) | copy-start | bytes 196612
  8.2 6.5 %copy-start.7 = (s32[2,24]{1,0:T(2,128)S(1)}, s32[2,24]{1,0:T(2,128)}, u32[]{:S(2)}) copy-start(s32[2,24]{1,0:T(2,128)} %rows.1) | copy-start | bytes 580
  8.2 6.5 %copy-start.8 = (s32[2,24]{1,0:T(2,128)S(1)}, s32[2,24]{1,0:T(2,128)}, u32[]{:S(2)}) copy-start(s32[2,24]{1,0:T(2,128)} %cols.1) | copy-start | bytes 580
  8.2 27.7 %all-to-all-start = ((bf16[4,24,128,128]{3,2,1,0:T(8,128)(2,1)}), bf16[4,24,128,128]{3,2,1,0:T(8,128)(2,1)}, u32[]{:S(2)}, u32[]{:S(2)}) async-start(bf16[4,24,128,128]{3,2,1,0:T(8,128)(2,1)} %bitcast.6), calls=%async_computation | async-start | bytes 6291456 | tf_op jit(solution)/shard_map/all_to_all | solution.py:352
  14.7 1.9 %copy-start.1 = (bf16[128,12288]{1,0:T(8,128)(2,1)S(1)}, bf16[128,12288]{1,0:T(8,128)(2,1)}, u32[]{:S(2)}) copy-start(bf16[128,12288]{1,0:T(8,128)(2,1)} %out_grad.1) | copy-start | bytes 9437188
  20.4 0.9 %copy-start.2 = (bf16[2,2,2,3,128,128]{5,4,3,2,1,0:T(8,128)(2,1)}, bf16[2,2,2,3,128,128]{5,4,3,2,1,0:T(8,128)(2,1)S(1)}, u32[]{:S(2)}) copy-start(bf16[2,2,2,3,128,128]{5,4,3,2,1,0:T(8,128)(2,1)S(1)} %get-tuple-element.20.refs_0_) | copy-start | bytes 2359300
  21.4 12.3 %collective-permute-start = (bf16[2,2,2,3,128,128]{5,4,3,2,1,0:T(8,128)(2,1)S(1)}, bf16[2,2,2,3,128,128]{5,4,3,2,1,0:T(8,128)(2,1)S(1)}, u32[]{:S(2)}, u32[]{:S(2)}) collective-permute-start(bf16[2,2,2,3,128,128]{5,4,3,2,1,0:T(8,128)(2,1)S(1)} %get-tuple-element.17), channel_id=1, source_target_pairs={{0,384},{384,0},{1,385},{385,1},{2,386},{386,2},{3,387},{387,3},{4... | collective-permute-start | bytes 2359304 | tf_op jit(solution)/shard_map/ppermute | solution.py:370
  31.8 4.2 %collective-permute-start.1 = (bf16[2,2,2,3,128,128]{5,4,3,2,1,0:T(8,128)(2,1)S(1)}, bf16[2,2,2,3,128,128]{5,4,3,2,1,0:T(8,128)(2,1)S(1)}, u32[]{:S(2)}, u32[]{:S(2)}) collective-permute-start(bf16[2,2,2,3,128,128]{5,4,3,2,1,0:T(8,128)(2,1)S(1)} %get-tuple-element.18), channel_id=1, source_target_pairs={{0,384},{384,0},{1,385},{385,1},{2,386},{386,2},{3,387},{387,3},{4... | collective-permute-start | bytes 2359304 | tf_op jit(solution)/shard_map/ppermute | solution.py:371
  33.9 0.9 %copy-start.4 = (bf16[2,2,2,3,128,128]{5,4,3,2,1,0:T(8,128)(2,1)}, bf16[2,2,2,3,128,128]{5,4,3,2,1,0:T(8,128)(2,1)S(1)}, u32[]{:S(2)}) copy-start(bf16[2,2,2,3,128,128]{5,4,3,2,1,0:T(8,128)(2,1)S(1)} %shard_map.105) | copy-start | bytes 2359300
  34.8 33.7 %copy-start.3 = (bf16[2,2,2,3,128,128]{5,4,3,2,1,0:T(8,128)(2,1)S(1)}, bf16[2,2,2,3,128,128]{5,4,3,2,1,0:T(8,128)(2,1)}, u32[]{:S(2)}) copy-start(bf16[2,2,2,3,128,128]{5,4,3,2,1,0:T(8,128)(2,1)} %copy-done.2) | copy-start | bytes 2359300
  38.6 23.0 %all-to-all-start.1 = ((bf16[4,6,128,128]{3,2,1,0:T(8,128)(2,1)}), bf16[4,6,128,128]{3,2,1,0:T(8,128)(2,1)S(1)}, u32[]{:S(2)}, u32[]{:S(2)}) async-start(bf16[4,6,128,128]{3,2,1,0:T(8,128)(2,1)} %bitcast.7), calls=%async_computation.1 | async-start | bytes 1572864 | tf_op jit(solution)/shard_map/all_to_all | solution.py:375
  52.9 15.5 %collective-permute-start.2 = (bf16[2,2,2,3,128,128]{5,4,3,2,1,0:T(8,128)(2,1)}, bf16[2,2,2,3,128,128]{5,4,3,2,1,0:T(8,128)(2,1)S(1)}, u32[]{:S(2)}, u32[]{:S(2)}) collective-permute-start(bf16[2,2,2,3,128,128]{5,4,3,2,1,0:T(8,128)(2,1)} %copy-done.4), channel_id=1, source_target_pairs={{0,96},{96,0},{192,288},{288,192},{384,672},{480,576},{576,480},{6... | collective-permute-start | bytes 2359304 | tf_op jit(solution)/shard_map/ppermute | solution.py:373
  62.3 20.5 %all-to-all-start.2 = ((bf16[6,128,128]{2,1,0:T(8,128)(2,1)}), bf16[6,128,128]{2,1,0:T(8,128)(2,1)S(1)}, u32[]{:S(2)}, u32[]{:S(2)}) async-start(bf16[6,128,128]{2,1,0:T(8,128)(2,1)} %shard_map.107), calls=%async_computation.2 | async-start | bytes 393216 | tf_op jit(solution)/shard_map/all_to_all | solution.py:387
  68.6 10.9 %collective-permute-start.3 = (bf16[1,2,2,3,128,128]{5,4,3,2,1,0:T(8,128)(2,1)S(1)}, bf16[1,2,2,3,128,128]{5,4,3,2,1,0:T(8,128)(2,1)S(1)}, u32[]{:S(2)}, u32[]{:S(2)}) collective-permute-start(bf16[1,2,2,3,128,128]{5,4,3,2,1,0:T(8,128)(2,1)S(1)} %shard_map.109), channel_id=1, source_target_pairs={{0,288},{96,192},{192,96},{288,0},{384,480},{480,384},{576,672},{6... | collective-permute-start | bytes 1179656 | tf_op jit(solution)/shard_map/ppermute | solution.py:382

commit v5 on v4

--- a/solution.py
+++ b/solution.py
@@ -66,12 +66,20 @@
 PLACE_Y, PLACE_Z = ring_place(N_Y, FAR_Y), ring_place(N_Z, FAR_Z)
 
 
+AROUND = (0, 3, 1, 2)
+
+
+def around(groups):
+    return [[group[i] for i in AROUND] for group in groups]
+
+
 def place_table():
     table = []
     for core in range(N_DP):
         for r in range(N_Y * N_Z):
             a, b = PLACE_Y[(r // N_Z - core) % N_Y], PLACE_Z[(r % N_Z - core) % N_Z]
-            table.append(((a[0] * 2 + b[0]) * 4 + a[1] * 2 + b[1]) * 6 + a[2] * 3 + b[2])
+            near, mid = AROUND.index(a[0] * 2 + b[0]), AROUND.index(a[1] * 2 + b[1])
+            table.append((near * 4 + mid) * 6 + a[2] * 3 + b[2])
     return table
 
 
@@ -350,7 +358,7 @@
     )
     everyone = TOKENS_AX + OWNER_AX
     near = lax.all_to_all(
-        placed.reshape(4, 24, BLK, tok), everyone, 0, 0, axis_index_groups=owner_groups(neighbours(N_Y, 0, 0), neighbours(N_Z, 0, 0))
+        placed.reshape(4, 24, BLK, tok), everyone, 0, 0, axis_index_groups=around(owner_groups(neighbours(N_Y, 0, 0), neighbours(N_Z, 0, 0)))
     )
 
     part_shape = jax.ShapeDtypeStruct((2, 2, slots, each, BLK, BLK), bf16)
@@ -377,7 +385,7 @@
         everyone,
         0,
         0,
-        axis_index_groups=owner_groups(neighbours(N_Y, 1, 1), neighbours(N_Z, 1, 1)),
+        axis_index_groups=around(owner_groups(neighbours(N_Y, 1, 1), neighbours(N_Z, 1, 1))),
     )
     second_got = lax.ppermute(
         add_last(1, mine_near, near_arrived, first_got),

time: 84 us -> 84 us (level)
  the two profiles are of different devices: /device:TPU:16 before, /device:TPU:20 now
where the time goes in v5:
time: 84 us; the launch traced here: 83.6 us
  starting transfers between devices  44.8 us (53%)
  waiting for transfers between devices  17.6 us (21%)
  Pallas kernels  16 us (19%)
  local copies, waits for them, and re-layouts  3.71 us (4%)
  between operations  1.45 us (2%)
    all_to_all x1, starting transfers between devices, local(): lax.all_to_all(sum_large(near).reshape(4, 6, BLK, tok), everyone, 0, 0, a...  14.3 us
    ppermute x1, starting transfers between devices, local(): far_arrived = lax.ppermute(theirs_far, 'dp', other_core)  10.4 us
    ppermute x1, waiting for transfers between devices, local(): lax.ppermute(add_last(1, mine_near, near_arrived, first_got), TOKENS_AX,...  7.23 us
    pallas_call x1, Pallas kernels, local(): pl.pallas_call(forward_kernel, out_shape=(jax.ShapeDtypeStruct((N_Y * N_Z...  6.87 us
    all_to_all x1, starting transfers between devices, local(): lax.all_to_all(placed.reshape(4, 24, BLK, tok), everyone, 0, 0, axis_inde...  6.46 us
    all_to_all x1, starting transfers between devices, local(): lax.all_to_all(sum_first(mid), everyone, 0, 0, axis_index_groups=owner_gr...  6.14 us
    all_to_all x1, waiting for transfers between devices, local(): lax.all_to_all(sum_large(near).reshape(4, 6, BLK, tok), everyone, 0, 0, a...  5.53 us
    pallas_call x1, Pallas kernels, local(): pl.pallas_call(weight_kernel, out_shape=(part_shape,) * 4, in_specs=[smem...  3.84 us
  transfers between devices with their start and end apart: 7, of which 4 were waited for; matrix products, arithmetic and copies ran while one was open for 0% of the time, Pallas kernels for 7%

profile of v5, /device:TPU:20, one launch (start us, length us, event | category | flops | bytes accessed | tf_op | source)
XLA Modules:
  0.0 83.6 jit_solution(14824987096067533385)
XLA Ops:
  1.3 6.9 %shard_map.103 = (bf16[96,128,128]{2,1,0:T(8,128)(2,1)}, bf16[2,128,128]{2,1,0:T(8,128)(2,1)}, bf16[2,128,128]{2,1,0:T(8,128)(2,1)}) custom-call(s32[1]{0:T(128)} %bitcast.core, s32[2,96]{1,0:T(2,128)} %constant.18.place_hbm, s32[2,24]{1,0:T(2,128)} %rows.1, s32[2,24]{1,0:T(2,128)} %cols.1, s32[1]{0:T(128)S(6)} %copy.11.count_hbm, ...), custom_call_target="tpu_custom_call" | custom-call | tf_op jit(solution)/shard_map/pallas_call | solution.py:322
  8.2 0.0 copy-start
  8.2 0.0 copy-start.5
  8.2 0.0 copy-start.6
  8.2 0.0 copy-start.7
  8.2 0.0 copy-start.8
  8.2 6.5 %all-to-all-start = ((bf16[4,24,128,128]{3,2,1,0:T(8,128)(2,1)}), bf16[4,24,128,128]{3,2,1,0:T(8,128)(2,1)}, u32[]{:S(2)}, u32[]{:S(2)}) async-start(bf16[4,24,128,128]{3,2,1,0:T(8,128)(2,1)} %bitcast.6), calls=%async_computation | async-start | bytes 6291456 | tf_op jit(solution)/shard_map/all_to_all | solution.py:360
  14.7 0.0 copy-done.7
  14.7 0.0 copy-start.1
  14.7 1.9 %copy-done.1 = bf16[128,12288]{1,0:T(8,128)(2,1)S(1)} copy-done((bf16[128,12288]{1,0:T(8,128)(2,1)S(1)}, bf16[128,12288]{1,0:T(8,128)(2,1)}, u32[]{:S(2)}) %copy-start.1) | copy-done | bytes 3145752
  16.6 3.8 %shard_map.104 = (bf16[2,2,2,3,128,128]{5,4,3,2,1,0:T(8,128)(2,1)S(1)}, bf16[2,2,2,3,128,128]{5,4,3,2,1,0:T(8,128)(2,1)S(1)}, bf16[2,2,2,3,128,128]{5,4,3,2,1,0:...) custom-call(s32[1]{0:T(128)} %bitcast.core, s32[1]{0:T(128)} %bitcast.4.seq, s32[2,24]{1,0:T(2,128)S(1)} %copy-done.7, ...), custom_call_target="tpu_custom_call" | custom-call | flops 400000000 | bytes 10000000 | tf_op jit(solution)/shard_map/pallas_call | solution.py:365
  20.5 0.9 %copy-done.2 = bf16[2,2,2,3,128,128]{5,4,3,2,1,0:T(8,128)(2,1)} copy-done((bf16[2,2,2,3,128,128]{5,4,3,2,1,0:T(8,128)(2,1)}, bf16[2,2,2,3,128,128]{5,4,3,2,1,0:T(8,128)(2,1)S(1)}, u32[]{:S(2)}) %copy-start.2) | copy-done | bytes 786456
  21.4 10.4 %collective-permute-start = (bf16[2,2,2,3,128,128]{5,4,3,2,1,0:T(8,128)(2,1)S(1)}, bf16[2,2,2,3,128,128]{5,4,3,2,1,0:T(8,128)(2,1)S(1)}, u32[]{:S(2)}, u32[]{:S(2)}) collective-permute-start(bf16[2,2,2,3,128,128]{5,4,3,2,1,0:T(8,128)(2,1)S(1)} %get-tuple-element.17), channel_id=1, source_target_pairs={{0,384},{384,0},{1,385},{385,1},{2,386},{386,2},{3,387},{387,3},{4... | collective-permute-start | bytes 2359304 | tf_op jit(solution)/shard_map/ppermute | solution.py:378
  31.8 1.9 %collective-permute-start.1 = (bf16[2,2,2,3,128,128]{5,4,3,2,1,0:T(8,128)(2,1)S(1)}, bf16[2,2,2,3,128,128]{5,4,3,2,1,0:T(8,128)(2,1)S(1)}, u32[]{:S(2)}, u32[]{:S(2)}) collective-permute-start(bf16[2,2,2,3,128,128]{5,4,3,2,1,0:T(8,128)(2,1)S(1)} %get-tuple-element.18), channel_id=1, source_target_pairs={{0,384},{384,0},{1,385},{385,1},{2,386},{386,2},{3,387},{387,3},{4... | collective-permute-start | bytes 2359304 | tf_op jit(solution)/shard_map/ppermute | solution.py:379
  33.7 0.0 collective-permute-done.refs_1_
  33.7 0.2 shard_map.105
  33.9 0.9 %copy-done.4 = bf16[2,2,2,3,128,128]{5,4,3,2,1,0:T(8,128)(2,1)} copy-done((bf16[2,2,2,3,128,128]{5,4,3,2,1,0:T(8,128)(2,1)}, bf16[2,2,2,3,128,128]{5,4,3,2,1,0:T(8,128)(2,1)S(1)}, u32[]{:S(2)}) %copy-start.4) | copy-done | bytes 786456
  34.8 1.2 %collective-permute-done.1.refs_1_ = bf16[2,2,2,3,128,128]{5,4,3,2,1,0:T(8,128)(2,1)S(1)} collective-permute-done((bf16[2,2,2,3,128,128]{5,4,3,2,1,0:T(8,128)(2,1)S(1)}, bf16[2,2,2,3,128,128]{5,4,3,2,1,0:T(8,128)(2,1)S(1)}, u32[]{:S(2)}, u32[]{:S(2)}) %collective-permute-start.1) | collective-permute-done | bytes 786464 | tf_op jit(solution)/shard_map/ppermute | solution.py:379
  35.9 0.0 all-to-all-done.terms_hbm
  36.0 2.6 %shard_map.106 = bf16[24,128,128]{2,1,0:T(8,128)(2,1)} custom-call(bf16[4,24,128,128]{3,2,1,0:T(8,128)(2,1)} %all-to-all-done.terms_hbm), custom_call_target="tpu_custom_call" | custom-call | tf_op jit(solution)/shard_map/pallas_call | solution.py:261
  38.6 14.3 %all-to-all-start.1 = ((bf16[4,6,128,128]{3,2,1,0:T(8,128)(2,1)}), bf16[4,6,128,128]{3,2,1,0:T(8,128)(2,1)S(1)}, u32[]{:S(2)}, u32[]{:S(2)}) async-start(bf16[4,6,128,128]{3,2,1,0:T(8,128)(2,1)} %bitcast.7), calls=%async_computation.1 | async-start | bytes 1572864 | tf_op jit(solution)/shard_map/all_to_all | solution.py:383
  52.9 3.1 %collective-permute-start.2 = (bf16[2,2,2,3,128,128]{5,4,3,2,1,0:T(8,128)(2,1)}, bf16[2,2,2,3,128,128]{5,4,3,2,1,0:T(8,128)(2,1)S(1)}, u32[]{:S(2)}, u32[]{:S(2)}) collective-permute-start(bf16[2,2,2,3,128,128]{5,4,3,2,1,0:T(8,128)(2,1)} %copy-done.4), channel_id=1, source_target_pairs={{0,96},{96,0},{192,288},{288,192},{384,672},{480,576},{576,480},{6... | collective-permute-start | bytes 2359304 | tf_op jit(solution)/shard_map/ppermute | solution.py:381
  56.0 5.5 %all-to-all-done.1.terms = bf16[4,6,128,128]{3,2,1,0:T(8,128)(2,1)S(1)} async-done(((bf16[4,6,128,128]{3,2,1,0:T(8,128)(2,1)}), bf16[4,6,128,128]{3,2,1,0:T(8,128)(2,1)S(1)}, u32[]{:S(2)}, u32[]{:S(2)}) %all-to-all-start.1) | async-done | bytes 786464 | tf_op jit(solution)/shard_map/all_to_all | solution.py:383
  61.5 0.8 shard_map.107
  62.3 6.1 %all-to-all-start.2 = ((bf16[6,128,128]{2,1,0:T(8,128)(2,1)}), bf16[6,128,128]{2,1,0:T(8,128)(2,1)S(1)}, u32[]{:S(2)}, u32[]{:S(2)}) async-start(bf16[6,128,128]{2,1,0:T(8,128)(2,1)} %shard_map.107), calls=%async_computation.2 | async-start | bytes 393216 | tf_op jit(solution)/shard_map/all_to_all | solution.py:395
  68.4 0.0 collective-permute-done.2.refs_2_
  68.4 0.1 shard_map.109
  68.6 2.4 %collective-permute-start.3 = (bf16[1,2,2,3,128,128]{5,4,3,2,1,0:T(8,128)(2,1)S(1)}, bf16[1,2,2,3,128,128]{5,4,3,2,1,0:T(8,128)(2,1)S(1)}, u32[]{:S(2)}, u32[]{:S(2)}) collective-permute-start(bf16[1,2,2,3,128,128]{5,4,3,2,1,0:T(8,128)(2,1)S(1)} %shard_map.109), channel_id=1, source_target_pairs={{0,288},{96,192},{192,96},{288,0},{384,480},{480,384},{576,672},{6... | collective-permute-start | bytes 1179656 | tf_op jit(solution)/shard_map/ppermute | solution.py:390
  71.0 7.2 %collective-permute-done.3.refs_3_ = bf16[1,2,2,3,128,128]{5,4,3,2,1,0:T(8,128)(2,1)S(1)} collective-permute-done((bf16[1,2,2,3,128,128]{5,4,3,2,1,0:T(8,128)(2,1)S(1)}, bf16[1,2,2,3,128,128]{5,4,3,2,1,0:T(8,128)(2,1)S(1)}, u32[]{:S(2)}, u32[]{:S(2)}) %collective-permute-start.3) | collective-permute-done | bytes 393248 | tf_op jit(solution)/shard_map/ppermute | solution.py:390
  78.3 0.9 %shard_map.110 = (bf16[2,3,128,128]{3,2,1,0:T(8,128)(2,1)}, bf16[2,3,128,128]{3,2,1,0:T(8,128)(2,1)}) custom-call(bf16[2,2,2,3,128,128]{5,4,3,2,1,0:T(8,128)(2,1)S(1)} %copy-done.3, bf16[2,2,2,3,128,128]{5,4,3,2,1,0:T(8,128)(2,1)S(1)} %collective-permute-done.1.refs_1_, bf16[2,2,2,3,128,128]{5,4,3,2,1,0:T(8,128)(2,1)S(1)} %collective-permute-done.2.refs_2_, ...), custom_call_target="tpu_custom_call" | custom-call | tf_op jit(solution)/shard_map/pallas_call | solution.py:215
  79.2 3.6 %all-to-all-done.2.terms = bf16[6,128,128]{2,1,0:T(8,128)(2,1)S(1)} async-done(((bf16[6,128,128]{2,1,0:T(8,128)(2,1)}), bf16[6,128,128]{2,1,0:T(8,128)(2,1)S(1)}, u32[]{:S(2)}, u32[]{:S(2)}) %all-to-all-start.2) | async-done | bytes 196640 | tf_op jit(solution)/shard_map/all_to_all | solution.py:395
  82.8 0.7 shard_map.108
  (8 shorter events, 0.0 us)
Async XLA Ops:
  8.2 6.5 %copy-start = (bf16[128,12288]{1,0:T(8,128)(2,1)S(1)}, bf16[128,12288]{1,0:T(8,128)(2,1)}, u32[]{:S(2)}) copy-start(bf16[128,12288]{1,0:T(8,128)(2,1)} %inputs.1) | copy-start | bytes 9437188
  8.2 6.5 %copy-start.5 = (bf16[2,128,128]{2,1,0:T(8,128)(2,1)S(1)}, bf16[2,128,128]{2,1,0:T(8,128)(2,1)}, u32[]{:S(2)}) copy-start(bf16[2,128,128]{2,1,0:T(8,128)(2,1)} %get-tuple-element.14.hidden_t) | copy-start | bytes 196612
  8.2 6.5 %copy-start.6 = (bf16[2,128,128]{2,1,0:T(8,128)(2,1)S(1)}, bf16[2,128,128]{2,1,0:T(8,128)(2,1)}, u32[]{:S(2)}) copy-start(bf16[2,128,128]{2,1,0:T(8,128)(2,1)} %get-tuple-element.15.pre_grad_t) | copy-start | bytes 196612
  8.2 6.5 %copy-start.7 = (s32[2,24]{1,0:T(2,128)S(1)}, s32[2,24]{1,0:T(2,128)}, u32[]{:S(2)}) copy-start(s32[2,24]{1,0:T(2,128)} %rows.1) | copy-start | bytes 580
  8.2 6.5 %copy-start.8 = (s32[2,24]{1,0:T(2,128)S(1)}, s32[2,24]{1,0:T(2,128)}, u32[]{:S(2)}) copy-start(s32[2,24]{1,0:T(2,128)} %cols.1) | copy-start | bytes 580
  8.2 27.7 %all-to-all-start = ((bf16[4,24,128,128]{3,2,1,0:T(8,128)(2,1)}), bf16[4,24,128,128]{3,2,1,0:T(8,128)(2,1)}, u32[]{:S(2)}, u32[]{:S(2)}) async-start(bf16[4,24,128,128]{3,2,1,0:T(8,128)(2,1)} %bitcast.6), calls=%async_computation | async-start | bytes 6291456 | tf_op jit(solution)/shard_map/all_to_all | solution.py:360
  14.7 1.9 %copy-start.1 = (bf16[128,12288]{1,0:T(8,128)(2,1)S(1)}, bf16[128,12288]{1,0:T(8,128)(2,1)}, u32[]{:S(2)}) copy-start(bf16[128,12288]{1,0:T(8,128)(2,1)} %out_grad.1) | copy-start | bytes 9437188
  20.4 0.9 %copy-start.2 = (bf16[2,2,2,3,128,128]{5,4,3,2,1,0:T(8,128)(2,1)}, bf16[2,2,2,3,128,128]{5,4,3,2,1,0:T(8,128)(2,1)S(1)}, u32[]{:S(2)}) copy-start(bf16[2,2,2,3,128,128]{5,4,3,2,1,0:T(8,128)(2,1)S(1)} %get-tuple-element.20.refs_0_) | copy-start | bytes 2359300
  21.4 12.3 %collective-permute-start = (bf16[2,2,2,3,128,128]{5,4,3,2,1,0:T(8,128)(2,1)S(1)}, bf16[2,2,2,3,128,128]{5,4,3,2,1,0:T(8,128)(2,1)S(1)}, u32[]{:S(2)}, u32[]{:S(2)}) collective-permute-start(bf16[2,2,2,3,128,128]{5,4,3,2,1,0:T(8,128)(2,1)S(1)} %get-tuple-element.17), channel_id=1, source_target_pairs={{0,384},{384,0},{1,385},{385,1},{2,386},{386,2},{3,387},{387,3},{4... | collective-permute-start | bytes 2359304 | tf_op jit(solution)/shard_map/ppermute | solution.py:378
  31.8 4.2 %collective-permute-start.1 = (bf16[2,2,2,3,128,128]{5,4,3,2,1,0:T(8,128)(2,1)S(1)}, bf16[2,2,2,3,128,128]{5,4,3,2,1,0:T(8,128)(2,1)S(1)}, u32[]{:S(2)}, u32[]{:S(2)}) collective-permute-start(bf16[2,2,2,3,128,128]{5,4,3,2,1,0:T(8,128)(2,1)S(1)} %get-tuple-element.18), channel_id=1, source_target_pairs={{0,384},{384,0},{1,385},{385,1},{2,386},{386,2},{3,387},{387,3},{4... | collective-permute-start | bytes 2359304 | tf_op jit(solution)/shard_map/ppermute | solution.py:379
  33.9 0.9 %copy-start.4 = (bf16[2,2,2,3,128,128]{5,4,3,2,1,0:T(8,128)(2,1)}, bf16[2,2,2,3,128,128]{5,4,3,2,1,0:T(8,128)(2,1)S(1)}, u32[]{:S(2)}) copy-start(bf16[2,2,2,3,128,128]{5,4,3,2,1,0:T(8,128)(2,1)S(1)} %shard_map.105) | copy-start | bytes 2359300
  34.8 33.7 %copy-start.3 = (bf16[2,2,2,3,128,128]{5,4,3,2,1,0:T(8,128)(2,1)S(1)}, bf16[2,2,2,3,128,128]{5,4,3,2,1,0:T(8,128)(2,1)}, u32[]{:S(2)}) copy-start(bf16[2,2,2,3,128,128]{5,4,3,2,1,0:T(8,128)(2,1)} %copy-done.2) | copy-start | bytes 2359300
  38.6 23.0 %all-to-all-start.1 = ((bf16[4,6,128,128]{3,2,1,0:T(8,128)(2,1)}), bf16[4,6,128,128]{3,2,1,0:T(8,128)(2,1)S(1)}, u32[]{:S(2)}, u32[]{:S(2)}) async-start(bf16[4,6,128,128]{3,2,1,0:T(8,128)(2,1)} %bitcast.7), calls=%async_computation.1 | async-start | bytes 1572864 | tf_op jit(solution)/shard_map/all_to_all | solution.py:383
  52.9 15.5 %collective-permute-start.2 = (bf16[2,2,2,3,128,128]{5,4,3,2,1,0:T(8,128)(2,1)}, bf16[2,2,2,3,128,128]{5,4,3,2,1,0:T(8,128)(2,1)S(1)}, u32[]{:S(2)}, u32[]{:S(2)}) collective-permute-start(bf16[2,2,2,3,128,128]{5,4,3,2,1,0:T(8,128)(2,1)} %copy-done.4), channel_id=1, source_target_pairs={{0,96},{96,0},{192,288},{288,192},{384,672},{480,576},{576,480},{6... | collective-permute-start | bytes 2359304 | tf_op jit(solution)/shard_map/ppermute | solution.py:381
  62.3 20.5 %all-to-all-start.2 = ((bf16[6,128,128]{2,1,0:T(8,128)(2,1)}), bf16[6,128,128]{2,1,0:T(8,128)(2,1)S(1)}, u32[]{:S(2)}, u32[]{:S(2)}) async-start(bf16[6,128,128]{2,1,0:T(8,128)(2,1)} %shard_map.107), calls=%async_computation.2 | async-start | bytes 393216 | tf_op jit(solution)/shard_map/all_to_all | solution.py:395
  68.6 9.7 %collective-permute-start.3 = (bf16[1,2,2,3,128,128]{5,4,3,2,1,0:T(8,128)(2,1)S(1)}, bf16[1,2,2,3,128,128]{5,4,3,2,1,0:T(8,128)(2,1)S(1)}, u32[]{:S(2)}, u32[]{:S(2)}) collective-permute-start(bf16[1,2,2,3,128,128]{5,4,3,2,1,0:T(8,128)(2,1)S(1)} %shard_map.109), channel_id=1, source_target_pairs={{0,288},{96,192},{192,96},{288,0},{384,480},{480,384},{576,672},{6... | collective-permute-start | bytes 1179656 | tf_op jit(solution)/shard_map/ppermute | solution.py:390
